TPU v7x, 32 devices: a whole 2x2x4 slice. The times are simulated.
32 devices in a mesh: dp: 2 (over x), fsdp: 16 (over z, y, core).
Axes of the slice: x: 2, y: 2, z: 4, core: 2. Of those that a mesh axis runs over, the one named last changes fastest.
Arguments:
- hidden: bfloat16 [8192, 8192], P(('dp', 'fsdp')), may hold values from -6 to 6
- lengths: int32 [128], P(('dp', 'fsdp')), may hold values from 16 to 112, as said below
- learner: int32 [128], P(('dp', 'fsdp')), may hold values from 0 to 1, as said below
- slot_offset: int32 [128], P(('dp', 'fsdp')), may hold values from 0 to 240, as said below
- norm_gain: bfloat16 [8192], P('fsdp'), may hold values from 0.099609375 to 1.8984375
- query_weight: bfloat16 [8192, 512], P('fsdp'), may hold values from -2 to 2
- keyval_weight: bfloat16 [8192, 256], P('fsdp'), may hold values from -2 to 2
Outputs:
- attended: bfloat16 [8192, 512], P(('dp', 'fsdp'))
Inputs may be any that keep to these rules, and one draw needn't show every extreme that they name: Rows 2k and 2k+1 of one device form a pair whose lengths sum to 128; a device's rows fill its 256 slots in order. Both rows of a pair go to the same learner; every learner receives exactly 2 pairs from the devices of its fsdp index. `slot_offset`: the rows that one learner receives tile its 256 slots without gaps, in some order.
All inputs are finite; a program needn't handle non-finite values.
Results may differ from a plain program's by a relative error of at most 0.0076.
Values may be sent and summed in bfloat16 or wider, within the bound.
A program may use at most 128 MiB of HBM per device.

v0:
```python
import jax
import jax.numpy as jnp
from jax import lax
from jax.sharding import PartitionSpec as P

HD = 128
QH = 4


rope_base = 500000.0
norm_eps = 1e-05


def rotate(values, positions):
    midpoint = values.shape[-1] // 2
    frequency = rope_base ** (-jnp.arange(midpoint, dtype=jnp.float32) * 2.0 / values.shape[-1])
    angles = positions.astype(jnp.float32)[:, None] * frequency[None, :]
    cosine = jnp.cos(angles)[:, None, :]
    sines = jnp.sin(angles)[:, None, :]
    leading = values[..., :midpoint]
    trailing = values[..., midpoint:]
    return jnp.concatenate(
        [leading * cosine - trailing * sines, trailing * cosine + leading * sines], -1
    )


def project(rows, positions, norm_gain, query_weight, keyval_weight):
    inverse = lax.rsqrt(
        jnp.mean(jnp.square(rows.astype(jnp.float32)), axis=1, keepdims=True) + norm_eps
    )
    gain_piece = lax.all_gather(norm_gain, "fsdp", axis=0, tiled=True)
    query_piece = lax.all_gather(query_weight, "fsdp", axis=0, tiled=True)
    kv_piece = lax.all_gather(keyval_weight, "fsdp", axis=0, tiled=True)
    normed = (rows.astype(jnp.float32) * inverse * gain_piece.astype(jnp.float32)[None, :]).astype(
        jnp.bfloat16
    )
    query = jnp.dot(normed, query_piece, preferred_element_type=jnp.float32)
    key_value = jnp.dot(normed, kv_piece, preferred_element_type=jnp.float32)
    query = rotate(query.reshape(-1, QH, HD), positions).reshape(-1, QH * HD)
    key_part = rotate(key_value[:, :HD].reshape(-1, 1, HD), positions).reshape(-1, HD)
    return jnp.concatenate([query, key_part, key_value[:, HD:]], axis=1).astype(jnp.bfloat16)


def source_positions(lengths, slot_count):
    starts = jnp.cumsum(lengths) - lengths
    places = jnp.arange(slot_count, dtype=jnp.int32)
    relative = places[:, None] - starts[None, :]
    inside = (relative >= 0) & (relative < lengths[None, :])
    return jnp.sum(jnp.where(inside, relative, 0), axis=1)


def route(buffer, tables):
    channels = buffer.shape[1]
    peer_count = lax.axis_size("dp")
    pair_count = tables.shape[1] // (2 * peer_count)
    block_len = buffer.shape[0] // pair_count
    slice_len = block_len // peer_count
    blocks = buffer.reshape(pair_count, peer_count, slice_len, channels)
    spread = lax.all_to_all(blocks, "dp", split_axis=1, concat_axis=0, tiled=True)
    lengths_all = tables[0].reshape(peer_count * pair_count, 2)
    targets = tables[1].reshape(peer_count * pair_count, 2)[:, 0]
    offsets_all = tables[2].reshape(peer_count * pair_count, 2)
    ordering = jnp.argsort(targets, stable=True)
    arranged = jnp.take(spread, ordering, axis=0).reshape(
        peer_count, pair_count, 1, slice_len, channels
    )
    received = lax.all_to_all(arranged, "dp", split_axis=0, concat_axis=2, tiled=True)
    received = received.reshape(pair_count * block_len, channels)
    own_blocks = lax.dynamic_slice_in_dim(ordering, lax.axis_index("dp") * pair_count, pair_count)
    pair_lengths = jnp.take(lengths_all, own_blocks, axis=0)
    sources = jnp.stack([jnp.zeros_like(pair_lengths[:, 0]), pair_lengths[:, 0]], axis=1)
    sources = (sources + (jnp.arange(pair_count, dtype=jnp.int32) * block_len)[:, None]).reshape(-1)
    row_lengths = pair_lengths.reshape(-1)
    row_offsets = jnp.take(offsets_all, own_blocks, axis=0).reshape(-1)
    places = jnp.arange(pair_count * block_len, dtype=jnp.int32)
    relative = places[:, None] - row_offsets[None, :]
    inside = (relative >= 0) & (relative < row_lengths[None, :])
    take_index = jnp.sum(jnp.where(inside, sources[None, :] + relative, 0), axis=1)
    segment = jnp.sum(
        jnp.where(inside, jnp.arange(2 * pair_count, dtype=jnp.int32)[None, :], 0), axis=1
    )
    position = jnp.sum(jnp.where(inside, relative, 0), axis=1)
    return (jnp.take(received, take_index, axis=0), segment, position)


def attend(packed, segment, position):
    query = packed[:, : QH * HD].reshape(-1, QH, HD)
    key_part = packed[:, QH * HD : QH * HD + HD]
    value_part = packed[:, QH * HD + HD :]
    scores = jnp.einsum(
        "qhd,kd->hqk", query, key_part, preferred_element_type=jnp.float32
    ) * HD ** (-0.5)
    allowed = (segment[:, None] == segment[None, :]) & (position[None, :] <= position[:, None])
    scores = jnp.where(allowed[None], scores, -1e30)
    row_max = jnp.max(scores, axis=2, keepdims=True)
    weights = jnp.exp(scores - row_max)
    row_total = jnp.sum(weights, axis=2, keepdims=True)
    probability = (weights / row_total).astype(jnp.bfloat16)
    mixed = jnp.einsum("hqk,kd->qhd", probability, value_part, preferred_element_type=jnp.float32)
    return mixed.reshape(-1, QH * HD).astype(jnp.bfloat16)


def shards(hidden, lengths, learner, slot_offset, norm_gain, query_weight, keyval_weight):
    tables = lax.all_gather(jnp.stack([lengths, learner, slot_offset]), "dp", axis=1, tiled=True)
    positions = source_positions(lengths, hidden.shape[0])
    packed = project(hidden, positions, norm_gain, query_weight, keyval_weight)
    packed, segment, position = route(packed, tables)
    return attend(packed, segment, position)


def solution(mesh):
    placed = (
        P(("dp", "fsdp"), None),
        P(("dp", "fsdp")),
        P(("dp", "fsdp")),
        P(("dp", "fsdp")),
        P("fsdp"),
        P("fsdp", None),
        P("fsdp", None),
    )
    return jax.shard_map(
        shards, mesh=mesh, in_specs=placed, out_specs=P(("dp", "fsdp"), None), check_vma=False
    )
```

profile of v0, /device:TPU:1, one launch (start us, length us, event | category | flops | bytes accessed | tf_op | source)
XLA Modules:
  0.0 178.1 jit_solution(2868411771055583003)
XLA Ops:
  6.5 0.0 all-gather.7.cloned.1.call-start
  6.5 0.7 all-gather.7.cloned.1.call-update
  7.3 0.0 all-gather.5.cloned.1.call-start
  7.3 0.7 all-gather.5.cloned.1.call-update
  8.0 0.7 add_bitcast_fusion
  8.7 0.1 copy.51
  8.8 3.7 %all-gather = s32[2,4,3]{2,1,0:T(4,128)S(1)} all-gather(s32[1,4,3]{2,1,0:T(4,128)S(1)} %bitcast.70), channel_id=1, replica_groups=mesh['dp'=2,'fsdp'=16] {'dp'}, dimensions={0}, use_global_device_ids=true | all-gather | bytes 144 | tf_op jit(solution)/shard_map/all_gather | solution.py:104
  12.5 0.7 reshape.319
  13.2 23.9 %all-gather.1 = bf16[16,1,512]{2,1,0:T(2,128)(2,1)S(1)} all-gather(bf16[1,1,512]{2,1,0:T(2,128)(2,1)S(1)} %reshape.319), channel_id=1, replica_groups=mesh['dp'=2,'fsdp'=16] {'fsdp'}, dimensions={0}, use_global_device_ids=true | all-gather | bytes 17408 | tf_op jit(solution)/shard_map/all_gather | solution.py:31
  37.1 0.8 reduce-window.9
  38.0 0.7 bitcast_subtract_fusion
  38.6 0.7 select_reduce_fusion.2
  39.4 0.1 copy.66
  39.5 0.1 reshape_squeeze.10
  39.6 0.1 slice_reduce_fusion
  39.7 0.8 sort.17
  40.5 0.1 broadcast_in_dim.80
  40.5 0.1 reshape_squeeze.9
  40.6 0.1 reshape_squeeze.11
  40.7 0.1 compare_and_fusion.1
  40.8 0.6 gather_fusion.2
  41.4 0.6 gather_fusion.3
  41.9 0.1 broadcast_select_fusion.2
  42.0 0.1 lt.50
  42.1 0.1 sub.46
  42.2 0.1 pad_add_fusion
  42.2 0.1 add.71
  42.3 0.1 select_reduce_fusion.1
  42.5 3.1 %fusion.1 = f32[256]{0:T(256)S(1)} fusion(bf16[256,8192]{1,0:T(8,128)(2,1)} %param.9), kind=kLoop, calls=%fused_computation.7 | loop fusion | flops 6291200 | bytes 4195328 | tf_op jit(solution)/shard_map/reduce_sum | solution.py:29
  45.6 0.5 multiply_cosine_fusion
  46.1 16.6 %all-gather.7.cloned.1.call-done = bf16[8192,256]{1,0:T(8,128)(2,1)} async-done(((bf16[512,256]{1,0:T(8,128)(2,1)}), bf16[8192,256]{1,0:T(8,128)(2,1)}) %all-gather.7.cloned.1.call-update) | async-done | bytes 4194320 | tf_op jit(solution)/shard_map/all_gather | solution.py:33
  62.7 5.6 %fusion.8 = f32[256,256]{0,1:T(8,128)S(1)} fusion(bf16[8192,256]{1,0:T(8,128)(2,1)} %all-gather.7.cloned.1.call-done, bf16[256,8192]{1,0:T(8,128)(2,1)} %param.9, f32[8192]{0:T(1024)S(1)} %bitcast.67, f32[256]{0:T(256)S(1)} %add_rsqrt_fusion), kind=kOutput, calls=%fused_computation.16 | convolution fusion | flops 1082130432 | bytes 8684544 | tf_op jit(solution)/shard_map/dot_general | solution.py:38
  68.3 0.1 copy.54
  68.5 0.3 fusion.17
  68.8 0.1 copy.53
  68.9 69.5 %all-gather.5.cloned.1.call-done = bf16[8192,512]{1,0:T(8,128)(2,1)} async-done(((bf16[512,512]{1,0:T(8,128)(2,1)}), bf16[8192,512]{1,0:T(8,128)(2,1)}) %all-gather.5.cloned.1.call-update) | async-done | bytes 8388624 | tf_op jit(solution)/shard_map/all_gather | solution.py:32
  138.4 7.0 %fusion.10 = f32[256,512]{1,0:T(8,128)S(1)} fusion(bf16[8192,512]{1,0:T(8,128)(2,1)} %all-gather.5.cloned.1.call-done, bf16[256,8192]{1,0:T(8,128)(2,1)} %param.9, f32[8192]{0:T(1024)S(1)} %bitcast.68, f32[256]{0:T(256)S(1)} %add_rsqrt_fusion), kind=kOutput, calls=%fused_computation.17 | convolution fusion | flops 2155872256 | bytes 13140992 | tf_op jit(solution)/shard_map/dot_general | solution.py:37
  145.4 0.2 reshape.272
  145.6 0.5 subtract_convert_fusion
  146.1 0.4 pad_maximum_fusion.1
  146.5 0.1 concatenate.20
  146.6 0.8 copy.55
  147.4 3.5 %all-to-all-start = ((bf16[2,2,64,768]{3,2,0,1:T(8,128)(2,1)}), bf16[2,2,64,768]{3,2,0,1:T(8,128)(2,1)S(1)}, u32[]{:S(2)}, u32[]{:S(2)}) async-start(bf16[2,2,64,768]{3,2,0,1:T(8,128)(2,1)} %copy.55), calls=%async_computation | async-start | bytes 786432 | tf_op jit(solution)/shard_map/all_to_all | solution.py:59
  150.9 0.1 compare_and_fusion
  151.0 6.3 %all-to-all-done = bf16[2,2,64,768]{3,2,0,1:T(8,128)(2,1)S(1)} async-done(((bf16[2,2,64,768]{3,2,0,1:T(8,128)(2,1)}), bf16[2,2,64,768]{3,2,0,1:T(8,128)(2,1)S(1)}, u32[]{:S(2)}, u32[]{:S(2)}) %all-to-all-start) | async-done | bytes 393248 | tf_op jit(solution)/shard_map/all_to_all | solution.py:59
  157.3 0.6 gather_fusion
  157.9 0.8 select_bitcast_fusion
  158.7 3.5 %all-to-all-start.1 = ((bf16[2,2,1,64,768]{4,3,1,2,0:T(8,128)(2,1)}), bf16[2,2,1,64,768]{4,3,1,2,0:T(8,128)(2,1)S(1)}, u32[]{:S(2)}, u32[]{:S(2)}) async-start(bf16[2,2,1,64,768]{4,3,1,2,0:T(8,128)(2,1)} %select_bitcast_fusion), calls=%async_computation.1 | async-start | bytes 786432 | tf_op jit(solution)/shard_map/all_to_all | solution.py:67
  162.2 5.5 %all-to-all-done.1 = bf16[2,2,1,64,768]{4,3,1,2,0:T(8,128)(2,1)S(1)} async-done(((bf16[2,2,1,64,768]{4,3,1,2,0:T(8,128)(2,1)}), bf16[2,2,1,64,768]{4,3,1,2,0:T(8,128)(2,1)S(1)}, u32[]{:S(2)}, u32[]{:S(2)}) %all-to-all-start.1) | async-done | bytes 393248 | tf_op jit(solution)/shard_map/all_to_all | solution.py:67
  167.7 1.2 gather_fusion.1
  168.9 0.1 broadcast_select_fusion
  169.1 0.1 copy.58
  169.2 0.5 fusion.29
  169.7 0.3 fusion.7
  170.0 0.4 convolution_convert_fusion
  170.4 0.8 copy.62
  (20 shorter events, 0.2 us)
Async XLA Ops:
  6.5 56.2 %all-gather.7.cloned.1.call-start = ((), (), s32[]{:S(2)}) async-start(), calls=%async_computation.3 | async-start | bytes 4456448 | tf_op jit(solution)/shard_map/all_gather | solution.py:33
  7.3 131.1 %all-gather.5.cloned.1.call-start = ((), (), s32[]{:S(2)}) async-start(), calls=%async_computation.2 | async-start | bytes 8912896 | tf_op jit(solution)/shard_map/all_gather | solution.py:32
  147.4 9.9 %all-to-all-start = ((bf16[2,2,64,768]{3,2,0,1:T(8,128)(2,1)}), bf16[2,2,64,768]{3,2,0,1:T(8,128)(2,1)S(1)}, u32[]{:S(2)}, u32[]{:S(2)}) async-start(bf16[2,2,64,768]{3,2,0,1:T(8,128)(2,1)} %copy.55), calls=%async_computation | async-start | bytes 786432 | tf_op jit(solution)/shard_map/all_to_all | solution.py:59
  158.7 9.0 %all-to-all-start.1 = ((bf16[2,2,1,64,768]{4,3,1,2,0:T(8,128)(2,1)}), bf16[2,2,1,64,768]{4,3,1,2,0:T(8,128)(2,1)S(1)}, u32[]{:S(2)}, u32[]{:S(2)}) async-start(bf16[2,2,1,64,768]{4,3,1,2,0:T(8,128)(2,1)} %select_bitcast_fusion), calls=%async_computation.1 | async-start | bytes 786432 | tf_op jit(solution)/shard_map/all_to_all | solution.py:67
Sparse Core Ops, SparseCore 0:
  9.5 53.1 all-gather.6
  64.9 73.4 all-gather.4
where the time goes:
time: 180 us; the launch traced here: 178 us
  waiting for transfers between devices  99.3 us (55%)
  blocking collectives  27.6 us (15%)
  matrix products  13.8 us (8%)
  between operations  13.6 us (8%)
  other arithmetic  10.1 us (6%)
  starting transfers between devices  6.97 us (4%)
  local copies, waits for them, and re-layouts  6.78 us (4%)
    all_gather x1, waiting for transfers between devices, project(): query_piece = lax.all_gather(query_weight, 'fsdp', axis=0, tiled=True)  69.5 us
    all_gather x1, blocking collectives, project(): gain_piece = lax.all_gather(norm_gain, 'fsdp', axis=0, tiled=True)  23.9 us
    all_gather x1, waiting for transfers between devices, project(): kv_piece = lax.all_gather(keyval_weight, 'fsdp', axis=0, tiled=True)  16.6 us
    dot_general x1, matrix products, project(): query = jnp.dot(normed, query_piece, preferred_element_type=jnp.float32)  7.02 us
    all_to_all x1, waiting for transfers between devices, route(): lax.all_to_all(blocks, 'dp', split_axis=1, concat_axis=0, tiled=True)  6.29 us
    dot_general x1, matrix products, project(): key_value = jnp.dot(normed, kv_piece, preferred_element_type=jnp.float32)  5.55 us
    all_to_all x1, waiting for transfers between devices, route(): lax.all_to_all(arranged, 'dp', split_axis=0, concat_axis=2, tiled=True)  5.5 us
    all_gather x1, blocking collectives, shards(): lax.all_gather(jnp.stack([lengths, learner, slot_offset]), 'dp', axis=1,...  3.73 us
  transfers between devices with their start and end apart: 4, of which 4 were waited for; matrix products, arithmetic and copies ran while one was open for 9% of the time, Pallas kernels for 0%

commit v1 on v0

v1 whole, which is shorter than its diff:
```python
import functools
import math

import jax
import jax.numpy as jnp
from jax import lax
from jax.experimental import pallas as pl
from jax.experimental.pallas import tpu as pltpu
from jax.sharding import PartitionSpec as P

HD = 128
QH = 4
ROPE_BASE = 500000.0
NORM_EPS = 1e-05
MESH = pl.DeviceIdType.MESH
PIECES = 4


def kernel(
    n_dp,
    n_fsdp,
    lengths_ref,
    learner_ref,
    offset_ref,
    hidden_ref,
    gain_ref,
    query_ref,
    keyval_ref,
    out_ref,
    weights,
    gains,
    own_rows,
    mate_rows,
    own_inv,
    mate_inv,
    total,
    mate_total,
    cosine,
    sine,
    masked,
    place_here,
    place_there,
    sent_heads,
    got_heads,
    local_sem,
    part_recv,
    z_send,
    y_send,
    x_send,
    gain_send,
    gain_recv,
    rows_send,
    rows_recv,
    inv_sem,
    sum_send,
    sum_recv,
    head_send,
    head_recv,
):
    dp = lax.axis_index("dp")
    fs = lax.axis_index("fsdp")
    core = lax.rem(fs, 2)
    y = lax.rem(fs // 2, 2)
    z = fs // 4
    n_z = n_fsdp // 4
    x = lax.rem(dp, 2)
    x_peer = {"dp": dp + 1 - 2 * x}
    mate = {"fsdp": fs + 1 - 2 * core}
    y_peer = {"fsdp": fs + 2 - 4 * y}
    tokens = own_rows.shape[0]
    depth = query_ref.shape[0]
    n_cols = weights.shape[2]
    q_cols = QH * HD
    part = depth // PIECES
    own = z * 2 + y
    n_shards = 2 * n_z
    role_a = 3 * x
    role_b = 1 + x
    role_c = 2 - x
    role_d = 3 - 3 * x

    load_q = pltpu.make_async_copy(query_ref, weights.at[own, :, pl.ds(0, q_cols)], local_sem.at[0])
    load_kv = pltpu.make_async_copy(
        keyval_ref, weights.at[own, :, pl.ds(q_cols, n_cols - q_cols)], local_sem.at[1]
    )
    load_rows = pltpu.make_async_copy(hidden_ref, own_rows, local_sem.at[2])
    load_q.start()
    load_kv.start()
    load_rows.start()
    gains[own] = jnp.broadcast_to(gain_ref[...].astype(jnp.float32), (8, depth))

    barrier = pltpu.get_barrier_semaphore()
    pl.semaphore_signal(barrier, inc=1, device_id=x_peer, device_id_type=MESH)
    pl.semaphore_signal(barrier, inc=1, device_id=mate, device_id_type=MESH)
    for step in range(1, n_shards):
        peer = lax.rem(own + step, n_shards)
        pl.semaphore_signal(
            barrier, inc=1, device_id={"fsdp": peer * 2 + core}, device_id_type=MESH
        )
    pl.semaphore_wait(barrier, n_shards + 1)

    def piece(slot, q):
        return weights.at[slot, pl.ds(pl.multiple_of(q * part, part), part), :]

    def send_z(zz, q, up):
        slot = zz * 2 + y
        step = 1 if up else -1
        return pltpu.make_async_remote_copy(
            src_ref=piece(slot, q),
            dst_ref=piece(slot, q),
            send_sem=z_send.at[1 if up else 0, zz, q],
            recv_sem=part_recv.at[slot, q],
            device_id={"fsdp": fs + 4 * step},
            device_id_type=MESH,
        )

    def send_y(zz, q):
        slot = zz * 2 + y
        return pltpu.make_async_remote_copy(
            src_ref=piece(slot, q),
            dst_ref=piece(slot, q),
            send_sem=y_send.at[zz, q],
            recv_sem=part_recv.at[slot, q],
            device_id=y_peer,
            device_id_type=MESH,
        )

    def send_x(slot, q):
        return pltpu.make_async_remote_copy(
            src_ref=piece(slot, q),
            dst_ref=piece(slot, q),
            send_sem=x_send.at[slot, q],
            recv_sem=part_recv.at[slot, q],
            device_id=x_peer,
            device_id_type=MESH,
        )

    def arrived(slot, q):
        send_x(slot, q).wait_recv()

    def send_gain(step):
        peer = lax.rem(own + step, n_shards)
        return pltpu.make_async_remote_copy(
            src_ref=gains.at[own],
            dst_ref=gains.at[own],
            send_sem=gain_send.at[step],
            recv_sem=gain_recv.at[own],
            device_id={"fsdp": peer * 2 + core},
            device_id_type=MESH,
        )

    def send_rows(s):
        start = pl.multiple_of((s * 2 + 1 - core) * depth, depth)
        return pltpu.make_async_remote_copy(
            src_ref=hidden_ref.at[:, pl.ds(start, depth)],
            dst_ref=mate_rows.at[s],
            send_sem=rows_send.at[s],
            recv_sem=rows_recv.at[s],
            device_id=mate,
            device_id_type=MESH,
        )

    send_inv = pltpu.make_async_remote_copy(
        src_ref=own_inv,
        dst_ref=mate_inv,
        send_sem=inv_sem.at[0],
        recv_sem=inv_sem.at[1],
        device_id=mate,
        device_id_type=MESH,
    )

    load_q.wait()
    load_kv.wait()
    for q in (role_a, role_b, role_c):
        pl.when(z < n_z - 1)(lambda q=q: send_z(z, q, True).start())
        pl.when(z > 0)(lambda q=q: send_z(z, q, False).start())
        send_y(z, q).start()
    send_y(z, role_d).start()
    for step in range(1, n_shards):
        send_gain(step).start()
    for s in range(n_shards):
        send_rows(s).start()

    load_rows.wait()
    width = own_rows.shape[1]

    def square(i, carry):
        rows = pl.ds(pl.multiple_of(i * 32, 32), 32)
        values = own_rows[rows, :].astype(jnp.float32)
        mean = jnp.sum(values * values, axis=1, keepdims=True) / width
        own_inv[rows, :] = jnp.broadcast_to(lax.rsqrt(mean + NORM_EPS), (32, 128))
        return carry

    lax.fori_loop(0, tokens // 32, square, 0)
    send_inv.start()

    n_rows = lengths_ref.shape[0]
    across = lax.broadcasted_iota(jnp.int32, (1, tokens), 1)
    down = lax.broadcasted_iota(jnp.int32, (tokens, 1), 0)
    row_across = jnp.zeros_like(across)
    row_down = jnp.zeros_like(down)
    start_down = jnp.zeros_like(down)
    target = jnp.zeros_like(across)
    goes_to = jnp.zeros_like(across)
    start = jnp.int32(0)
    for r in range(n_rows):
        in_across = across >= start
        in_down = down >= start
        row_across = jnp.where(in_across, r, row_across)
        row_down = jnp.where(in_down, r, row_down)
        start_down = jnp.where(in_down, start, start_down)
        target = jnp.where(in_across, offset_ref[r] + across - start, target)
        goes_to = jnp.where(in_across, learner_ref[r], goes_to)
        start = start + lengths_ref[r]
    position = (down - start_down).astype(jnp.float32)
    lane = lax.broadcasted_iota(jnp.int32, (1, HD), 1)
    half = HD // 2
    index = jnp.where(lane < half, lane, lane - half).astype(jnp.float32)
    angle = position * jnp.exp(index * (-2.0 * math.log(ROPE_BASE) / HD))
    cosine[...] = jnp.cos(angle)
    sine[...] = jnp.where(lane < half, -jnp.sin(angle), jnp.sin(angle))
    allowed = (row_across == row_down) & (across <= down)
    masked[...] = jnp.where(allowed, 0.0, 1.0)
    if n_dp == 2:
        slot_iota = lax.broadcasted_iota(jnp.int32, (tokens, tokens), 0)
        place_here[...] = jnp.where(
            slot_iota == jnp.where(goes_to == dp, target, -1), 1.0, 0.0
        ).astype(jnp.bfloat16)
        place_there[...] = jnp.where(
            slot_iota == jnp.where(goes_to == 1 - dp, target, -1), 1.0, 0.0
        ).astype(jnp.bfloat16)

    def project(slot, first=False):
        gain = gains[slot][0:1, :]
        column = pl.multiple_of((slot * 2 + core) * depth, depth)
        mine = own_rows[:, pl.ds(column, depth)].astype(jnp.float32)
        normed = (mine * own_inv[:, 0:1] * gain).astype(jnp.bfloat16)
        result = jnp.dot(normed, weights[slot], preferred_element_type=jnp.float32)
        total[0] = result if first else total[0] + result
        theirs = mate_rows[slot].astype(jnp.float32)
        normed = (theirs * mate_inv[:, 0:1] * gain).astype(jnp.bfloat16)
        result = jnp.dot(normed, weights[slot], preferred_element_type=jnp.float32)
        total[1] = result if first else total[1] + result

    def sides(d):
        return ((z + d < n_z, z + d, False), (z - d >= 0, z - d, True))

    def along_z(d, q, to_y, to_x):
        for valid, zz, up in sides(d):

            @pl.when(valid)
            def _(zz=zz, up=up):
                arrived(zz * 2 + y, q)
                pl.when(z < n_z - 1 if up else z > 0)(lambda: send_z(zz, q, up).start())
                if to_y:
                    send_y(zz, q).start()
                if to_x:
                    send_x(zz * 2 + y, q).start()

    def along_y(d, q):
        for valid, zz, _ in sides(d):

            @pl.when(valid)
            def _(zz=zz):
                slot = zz * 2 + 1 - y
                arrived(slot, q)
                send_x(slot, q).start()

    def finish(d):
        for valid, zz, _ in sides(d):

            @pl.when(valid)
            def _(zz=zz):
                arrived(zz * 2 + y, role_d)
                arrived(zz * 2 + 1 - y, role_d)
                arrived(zz * 2 + 1 - y, role_c)

                def one(i, carry):
                    project(zz * 2 + i)
                    return carry

                lax.fori_loop(0, 2, one, 0)

    for step in range(1, n_shards):
        peer = lax.rem(own + step, n_shards)
        pltpu.make_async_remote_copy(
            src_ref=gains.at[peer],
            dst_ref=gains.at[peer],
            send_sem=gain_send.at[step],
            recv_sem=gain_recv.at[peer],
            device_id=mate,
            device_id_type=MESH,
        ).wait_recv()
    send_inv.wait_recv()
    for s in range(n_shards):
        send_rows(s).wait_recv()

    along_z(1, role_a, True, True)
    project(own, first=True)
    along_z(1, role_b, True, False)
    along_z(1, role_c, False, False)
    for q in range(PIECES):
        arrived(z * 2 + 1 - y, q)
    project(z * 2 + 1 - y)
    for d in range(2, n_z):
        along_z(d, role_a, True, True)
        along_y(d - 1, role_a)
        along_z(d, role_b, True, False)
        along_y(d - 1, role_b)
        along_z(d, role_c, False, False)
        if d > 2:
            finish(d - 2)
    along_y(n_z - 1, role_a)
    along_y(n_z - 1, role_b)
    for d in range(max(1, n_z - 2), n_z):
        finish(d)

    def send_sum(c):
        cols = pl.ds(c * 256, 256)
        return pltpu.make_async_remote_copy(
            src_ref=total.at[1, :, cols],
            dst_ref=mate_total.at[:, cols],
            send_sem=sum_send.at[c],
            recv_sem=sum_recv.at[c],
            device_id=mate,
            device_id_type=MESH,
        )

    n_sums = n_cols // 256
    order = [n_sums - 1] + list(range(n_sums - 1))
    for c in order:
        send_sum(c).start()

    def rotated(values):
        return (values * cosine[...] + pltpu.roll(values, half, 1) * sine[...]).astype(jnp.bfloat16)

    def summed(col):
        return total[0, :, col : col + HD] + mate_total[:, col : col + HD]

    send_sum(n_sums - 1).wait_recv()
    key = rotated(summed(q_cols))
    value = summed(q_cols + HD).astype(jnp.bfloat16)

    def send_head(h):
        return pltpu.make_async_remote_copy(
            src_ref=sent_heads.at[h],
            dst_ref=got_heads.at[h],
            send_sem=head_send.at[h],
            recv_sem=head_recv.at[h],
            device_id=x_peer,
            device_id_type=MESH,
        )

    for h in range(QH):
        if h % 2 == 0:
            send_sum(h // 2).wait_recv()
        query = rotated(summed(h * HD))
        scores = lax.dot_general(
            query, key, (((1,), (1,)), ((), ())), preferred_element_type=jnp.float32
        ) * HD ** (-0.5)
        scores = jnp.where(masked[...] > 0.5, -1e30, scores)
        exped = jnp.exp(scores - jnp.max(scores, axis=1, keepdims=True))
        chance = (exped / jnp.sum(exped, axis=1, keepdims=True)).astype(jnp.bfloat16)
        mixed = jnp.dot(chance, value, preferred_element_type=jnp.float32).astype(jnp.bfloat16)
        cols = pl.ds(h * HD, HD)
        if n_dp == 2:
            sent_heads[h] = jnp.dot(
                place_there[...], mixed, preferred_element_type=jnp.float32
            ).astype(jnp.bfloat16)
            send_head(h).start()
            out_ref[:, cols] = jnp.dot(
                place_here[...], mixed, preferred_element_type=jnp.float32
            ).astype(jnp.bfloat16)
        else:
            out_ref[:, cols] = mixed

    for q in (role_a, role_b, role_c):
        pl.when(z < n_z - 1)(lambda q=q: send_z(z, q, True).wait_send())
        pl.when(z > 0)(lambda q=q: send_z(z, q, False).wait_send())
        send_y(z, q).wait_send()
    send_y(z, role_d).wait_send()
    for step in range(1, n_shards):
        send_gain(step).wait_send()
    for s in range(n_shards):
        send_rows(s).wait_send()
    send_inv.wait_send()
    for d in range(1, n_z):
        for valid, zz, up in sides(d):

            @pl.when(valid)
            def _(zz=zz, up=up):
                for q in (role_a, role_b, role_c):
                    pl.when(z < n_z - 1 if up else z > 0)(
                        lambda q=q: send_z(zz, q, up).wait_send()
                    )
                send_y(zz, role_a).wait_send()
                send_y(zz, role_b).wait_send()
                send_x(zz * 2 + y, role_a).wait_send()
                send_x(zz * 2 + 1 - y, role_a).wait_send()
                send_x(zz * 2 + 1 - y, role_b).wait_send()

    for c in order:
        send_sum(c).wait_send()
    if n_dp == 2:
        for h in range(QH):
            cols = pl.ds(h * HD, HD)
            send_head(h).wait_recv()
            out_ref[:, cols] = out_ref[:, cols] + got_heads[h]
        for h in range(QH):
            send_head(h).wait_send()


def fused(n_dp, n_fsdp, hidden, lengths, learner, slot_offset, norm_gain, query_weight, keyval_weight):
    tokens, width = hidden.shape
    depth, q_cols = query_weight.shape
    n_cols = q_cols + keyval_weight.shape[1]
    n_z = n_fsdp // 4
    n_shards = 2 * n_z
    bf16, f32 = jnp.bfloat16, jnp.float32
    dma = pltpu.SemaphoreType.DMA
    smem = pl.BlockSpec(memory_space=pltpu.SMEM)
    vmem = pl.BlockSpec(memory_space=pltpu.VMEM)
    anywhere = pl.BlockSpec(memory_space=pl.ANY)
    return pl.pallas_call(
        functools.partial(kernel, n_dp, n_fsdp),
        out_shape=jax.ShapeDtypeStruct((tokens, q_cols), bf16),
        in_specs=[smem, smem, smem, anywhere, vmem, anywhere, anywhere],
        out_specs=vmem,
        scratch_shapes=[
            pltpu.VMEM((n_shards, depth, n_cols), bf16),
            pltpu.VMEM((n_shards, 8, depth), f32),
            pltpu.VMEM((tokens, width), bf16),
            pltpu.VMEM((n_shards, tokens, depth), bf16),
            pltpu.VMEM((tokens, 128), f32),
            pltpu.VMEM((tokens, 128), f32),
            pltpu.VMEM((2, tokens, n_cols), f32),
            pltpu.VMEM((tokens, n_cols), f32),
            pltpu.VMEM((tokens, HD), f32),
            pltpu.VMEM((tokens, HD), f32),
            pltpu.VMEM((tokens, tokens), f32),
            pltpu.VMEM((tokens, tokens), bf16),
            pltpu.VMEM((tokens, tokens), bf16),
            pltpu.VMEM((QH, tokens, HD), bf16),
            pltpu.VMEM((QH, tokens, HD), bf16),
            dma((3,)),
            dma((n_shards, PIECES)),
            dma((2, n_z, PIECES)),
            dma((n_z, PIECES)),
            dma((n_shards, PIECES)),
            dma((n_shards,)),
            dma((n_shards,)),
            dma((n_shards,)),
            dma((n_shards,)),
            dma((2,)),
            dma((n_cols // 256,)),
            dma((n_cols // 256,)),
            dma((QH,)),
            dma((QH,)),
        ],
        compiler_params=pltpu.CompilerParams(
            collective_id=0, has_side_effects=True, vmem_limit_bytes=48 * 1024 * 1024
        ),
    )(lengths, learner, slot_offset, hidden, norm_gain.reshape(1, -1), query_weight, keyval_weight)


def route(buffer, tables):
    channels = buffer.shape[1]
    peer_count = lax.axis_size("dp")
    pair_count = tables.shape[1] // (2 * peer_count)
    block_len = buffer.shape[0] // pair_count
    slice_len = block_len // peer_count
    blocks = buffer.reshape(pair_count, peer_count, slice_len, channels)
    spread = lax.all_to_all(blocks, "dp", split_axis=1, concat_axis=0, tiled=True)
    lengths_all = tables[0].reshape(peer_count * pair_count, 2)
    targets = tables[1].reshape(peer_count * pair_count, 2)[:, 0]
    offsets_all = tables[2].reshape(peer_count * pair_count, 2)
    ordering = jnp.argsort(targets, stable=True)
    arranged = jnp.take(spread, ordering, axis=0).reshape(
        peer_count, pair_count, 1, slice_len, channels
    )
    received = lax.all_to_all(arranged, "dp", split_axis=0, concat_axis=2, tiled=True)
    received = received.reshape(pair_count * block_len, channels)
    own_blocks = lax.dynamic_slice_in_dim(ordering, lax.axis_index("dp") * pair_count, pair_count)
    pair_lengths = jnp.take(lengths_all, own_blocks, axis=0)
    sources = jnp.stack([jnp.zeros_like(pair_lengths[:, 0]), pair_lengths[:, 0]], axis=1)
    sources = (sources + (jnp.arange(pair_count, dtype=jnp.int32) * block_len)[:, None]).reshape(-1)
    row_lengths = pair_lengths.reshape(-1)
    row_offsets = jnp.take(offsets_all, own_blocks, axis=0).reshape(-1)
    places = jnp.arange(pair_count * block_len, dtype=jnp.int32)
    relative = places[:, None] - row_offsets[None, :]
    inside = (relative >= 0) & (relative < row_lengths[None, :])
    take_index = jnp.sum(jnp.where(inside, sources[None, :] + relative, 0), axis=1)
    return jnp.take(received, take_index, axis=0)


def solution(mesh):
    n_dp, n_fsdp = mesh.shape["dp"], mesh.shape["fsdp"]

    def shards(hidden, lengths, learner, slot_offset, norm_gain, query_weight, keyval_weight):
        attended = fused(
            n_dp, n_fsdp, hidden, lengths, learner, slot_offset, norm_gain, query_weight, keyval_weight
        )
        if n_dp == 2:
            return attended
        tables = lax.all_gather(
            jnp.stack([lengths, learner, slot_offset]), "dp", axis=1, tiled=True
        )
        return route(attended, tables)

    placed = (
        P(("dp", "fsdp"), None),
        P(("dp", "fsdp")),
        P(("dp", "fsdp")),
        P(("dp", "fsdp")),
        P("fsdp"),
        P("fsdp", None),
        P("fsdp", None),
    )
    return jax.shard_map(
        shards, mesh=mesh, in_specs=placed, out_specs=P(("dp", "fsdp"), None), check_vma=False
    )
```

time: 180 us -> 84 us (0.47)
  waiting for transfers between devices: 99.3 us -> 0 us
  Pallas kernels: 0 us -> 76.2 us
  blocking collectives: 27.6 us -> 0 us
  matrix products: 13.8 us -> 0 us
  between operations: 13.6 us -> 0.02 us
  other arithmetic: 10.1 us -> 0 us
  starting transfers between devices: 6.97 us -> 0 us
    all_gather x2 -> x0, waiting for transfers between devices: 86.1 us -> none  [the longest x1 69.5 us: project(): query_piece = lax.all_gather(query_weight, 'fsdp', axis=0, tiled=True)]
    pallas_call x0 -> x1, Pallas kernels: none -> 76.2 us  [fused(): pl.pallas_call(functools.partial(kernel, n_dp, n_fsdp), out_shape=jax.Sha...]
    all_gather x2 -> x0, blocking collectives: 27.6 us -> none  [the longest x1 23.9 us: project(): gain_piece = lax.all_gather(norm_gain, 'fsdp', axis=0, tiled=True)]
    dot_general x4 -> x0, matrix products: 13.3 us -> none  [the longest x1 7.02 us: project(): query = jnp.dot(normed, query_piece, preferred_element_type=jnp.float32)]
    all_to_all x2 -> x0, waiting for transfers between devices: 11.8 us -> none  [the longest x1 6.29 us: route(): lax.all_to_all(blocks, 'dp', split_axis=1, concat_axis=0, tiled=True)]
    all_to_all x2 -> x0, starting transfers between devices: 6.93 us -> none  [the longest x1 3.46 us: route(): lax.all_to_all(blocks, 'dp', split_axis=1, concat_axis=0, tiled=True)]
    unnamed x3 -> x13, local copies, waits for them, and re-layouts: 0.86 us -> 6.85 us
    reduce_sum x3 -> x0, other arithmetic: 3.94 us -> none  [the longest x1 3.11 us: project(): jnp.mean(jnp.square(rows.astype(jnp.float32)), axis=1, keepdims=True)]
  transfers between devices with their start and end apart: 4 -> 0, of which waited for: 4 -> 0; matrix products, arithmetic and copies ran while one was open for 9% -> 0% of each run, Pallas kernels for 0% -> 0%
where the time goes in v1:
time: 84 us; the launch traced here: 83.8 us
  Pallas kernels  76.2 us (91%)
  local copies, waits for them, and re-layouts  7.53 us (9%)
    pallas_call x1, Pallas kernels, fused(): pl.pallas_call(functools.partial(kernel, n_dp, n_fsdp), out_shape=jax.Sha...  76.2 us
    unnamed x13, local copies, waits for them, and re-layouts  6.85 us

profile of v1, /device:TPU:1, one launch (start us, length us, event | category | flops | bytes accessed | tf_op | source)
XLA Modules:
  0.0 83.8 jit_solution(12450565204978612487)
XLA Ops:
  0.0 0.7 reshape.3.gain_ref
  0.7 0.0 copy-start
  0.7 2.2 %copy-done = bf16[256,8192]{1,0:T(8,128)(2,1)S(1)} copy-done((bf16[256,8192]{1,0:T(8,128)(2,1)S(1)}, bf16[256,8192]{1,0:T(8,128)(2,1)}, u32[]{:S(2)}) %copy-start) | copy-done | bytes 4194328
  2.9 0.0 copy-start.1
  2.9 1.0 %copy-done.1 = bf16[512,512]{1,0:T(8,128)(2,1)S(1)} copy-done((bf16[512,512]{1,0:T(8,128)(2,1)S(1)}, bf16[512,512]{1,0:T(8,128)(2,1)}, u32[]{:S(2)}) %copy-start.1) | copy-done | bytes 524312
  3.9 0.0 copy-start.2
  3.9 0.9 %copy-done.2 = bf16[512,256]{1,0:T(8,128)(2,1)S(1)} copy-done((bf16[512,256]{1,0:T(8,128)(2,1)S(1)}, bf16[512,256]{1,0:T(8,128)(2,1)}, u32[]{:S(2)}) %copy-start.2) | copy-done | bytes 262168
  4.9 0.0 copy-start.3
  4.9 0.7 copy-done.3
  5.5 0.0 copy-start.4
  5.5 0.7 copy-done.4
  6.2 0.0 copy-start.5
  6.2 0.7 copy-done.5
  6.8 76.2 %shard_map.73 = bf16[256,512]{1,0:T(8,128)(2,1)S(1)} custom-call(s32[4]{0:T(128)S(1)} %copy-done.3, s32[4]{0:T(128)S(1)} %copy-done.4, s32[4]{0:T(128)S(1)} %copy-done.5, bf16[256,8192]{1,0:T(8,128)(2,1)S(1)} %copy-done, bf16[1,512]{1,0:T(2,128)(2,1)S(1)} %reshape.3.gain_ref, bf16[512,512]{1,0:T(8,128)(2,1)S(1)} %copy-done.1, bf16[512,256]{1,0:T(8,128)(2,1)S(1)} %copy-done.2), custom_call_target="tpu_custom_call" | custom-call | tf_op jit(solution)/shard_map/pallas_call | solution.py:424
  83.1 0.7 copy.9
Async XLA Ops:
  0.7 2.2 %copy-start = (bf16[256,8192]{1,0:T(8,128)(2,1)S(1)}, bf16[256,8192]{1,0:T(8,128)(2,1)}, u32[]{:S(2)}) copy-start(bf16[256,8192]{1,0:T(8,128)(2,1)} %hidden_ref.1) | copy-start | bytes 12582916
  2.9 1.0 %copy-start.1 = (bf16[512,512]{1,0:T(8,128)(2,1)S(1)}, bf16[512,512]{1,0:T(8,128)(2,1)}, u32[]{:S(2)}) copy-start(bf16[512,512]{1,0:T(8,128)(2,1)} %query_ref.1) | copy-start | bytes 1572868
  3.9 0.9 %copy-start.2 = (bf16[512,256]{1,0:T(8,128)(2,1)S(1)}, bf16[512,256]{1,0:T(8,128)(2,1)}, u32[]{:S(2)}) copy-start(bf16[512,256]{1,0:T(8,128)(2,1)} %keyval_ref.1) | copy-start | bytes 786436
  4.9 0.7 copy-start.3
  5.5 0.7 copy-start.4
  6.2 0.7 copy-start.5

commit v2 on v1

--- a/solution.py
+++ b/solution.py
@@ -13,20 +13,23 @@
 ROPE_BASE = 500000.0
 NORM_EPS = 1e-05
 MESH = pl.DeviceIdType.MESH
-PIECES = 4
+SUBS = 2
 
 
 def kernel(
     n_dp,
     n_fsdp,
-    lengths_ref,
-    learner_ref,
-    offset_ref,
+    lengths_hbm,
+    learner_hbm,
+    offset_hbm,
     hidden_ref,
     gain_ref,
     query_ref,
     keyval_ref,
     out_ref,
+    lengths_ref,
+    learner_ref,
+    offset_ref,
     weights,
     gains,
     own_rows,
@@ -71,8 +74,9 @@
     depth = query_ref.shape[0]
     n_cols = weights.shape[2]
     q_cols = QH * HD
-    part = depth // PIECES
+    part = depth // (4 * SUBS)
     own = z * 2 + y
+    other = z * 2 + 1 - y
     n_shards = 2 * n_z
     role_a = 3 * x
     role_b = 1 + x
@@ -84,10 +88,17 @@
         keyval_ref, weights.at[own, :, pl.ds(q_cols, n_cols - q_cols)], local_sem.at[1]
     )
     load_rows = pltpu.make_async_copy(hidden_ref, own_rows, local_sem.at[2])
+    load_tables = [
+        pltpu.make_async_copy(src, dst, local_sem.at[3 + i])
+        for i, (src, dst) in enumerate(
+            ((lengths_hbm, lengths_ref), (learner_hbm, learner_ref), (offset_hbm, offset_ref))
+        )
+    ]
     load_q.start()
     load_kv.start()
     load_rows.start()
-    gains[own] = jnp.broadcast_to(gain_ref[...].astype(jnp.float32), (8, depth))
+    for load in load_tables:
+        load.start()
 
     barrier = pltpu.get_barrier_semaphore()
     pl.semaphore_signal(barrier, inc=1, device_id=x_peer, device_id_type=MESH)
@@ -97,46 +108,49 @@
         pl.semaphore_signal(
             barrier, inc=1, device_id={"fsdp": peer * 2 + core}, device_id_type=MESH
         )
+    gains[own] = jnp.broadcast_to(gain_ref[...].astype(jnp.float32).reshape(1, depth), (8, depth))
     pl.semaphore_wait(barrier, n_shards + 1)
 
-    def piece(slot, q):
-        return weights.at[slot, pl.ds(pl.multiple_of(q * part, part), part), :]
-
-    def send_z(zz, q, up):
+    def piece(slot, p):
+        return weights.at[slot, pl.ds(pl.multiple_of(p * part, part), part), :]
+
+    def send_z(zz, p, up):
         slot = zz * 2 + y
-        step = 1 if up else -1
-        return pltpu.make_async_remote_copy(
-            src_ref=piece(slot, q),
-            dst_ref=piece(slot, q),
-            send_sem=z_send.at[1 if up else 0, zz, q],
-            recv_sem=part_recv.at[slot, q],
-            device_id={"fsdp": fs + 4 * step},
-            device_id_type=MESH,
-        )
-
-    def send_y(zz, q):
+        return pltpu.make_async_remote_copy(
+            src_ref=piece(slot, p),
+            dst_ref=piece(slot, p),
+            send_sem=z_send.at[up, zz, p],
+            recv_sem=part_recv.at[slot, p],
+            device_id={"fsdp": fs + 8 * up - 4},
+            device_id_type=MESH,
+        )
+
+    def can_send(up):
+        return (z + 2 * up - 1 >= 0) & (z + 2 * up - 1 < n_z)
+
+    def send_y(zz, p):
         slot = zz * 2 + y
         return pltpu.make_async_remote_copy(
-            src_ref=piece(slot, q),
-            dst_ref=piece(slot, q),
-            send_sem=y_send.at[zz, q],
-            recv_sem=part_recv.at[slot, q],
+            src_ref=piece(slot, p),
+            dst_ref=piece(slot, p),
+            send_sem=y_send.at[zz, p],
+            recv_sem=part_recv.at[slot, p],
             device_id=y_peer,
             device_id_type=MESH,
         )
 
-    def send_x(slot, q):
-        return pltpu.make_async_remote_copy(
-            src_ref=piece(slot, q),
-            dst_ref=piece(slot, q),
-            send_sem=x_send.at[slot, q],
-            recv_sem=part_recv.at[slot, q],
+    def send_x(slot, p):
+        return pltpu.make_async_remote_copy(
+            src_ref=piece(slot, p),
+            dst_ref=piece(slot, p),
+            send_sem=x_send.at[slot, p],
+            recv_sem=part_recv.at[slot, p],
             device_id=x_peer,
             device_id_type=MESH,
         )
 
-    def arrived(slot, q):
-        send_x(slot, q).wait_recv()
+    def arrived(slot, p):
+        send_x(slot, p).wait_recv()
 
     def send_gain(step):
         peer = lax.rem(own + step, n_shards)
@@ -169,13 +183,62 @@
         device_id_type=MESH,
     )
 
+    def each(count, body):
+        def step(i, carry):
+            body(i)
+            return carry
+
+        lax.fori_loop(0, count, step, 0)
+
+    def own_z(q, act):
+        def body(j):
+            up = lax.rem(j, 2)
+            pl.when(can_send(up))(lambda: act(send_z(z, q * SUBS + j // 2, up)))
+
+        each(2 * SUBS, body)
+
+    def own_y(q, act):
+        each(SUBS, lambda j: act(send_y(z, q * SUBS + j)))
+
+    def start(copy):
+        copy.start()
+
+    def sent(copy):
+        copy.wait_send()
+
+    def remote(d, body):
+        def step(j):
+            up = lax.rem(j, 2)
+            zz = z + d - 2 * d * up
+            pl.when((zz >= 0) & (zz < n_z))(lambda: body(j // 2, zz, up))
+
+        each(2 * SUBS, step)
+
+    def along_z(d, q, to_y, to_x):
+        def body(sub, zz, up):
+            p = q * SUBS + sub
+            arrived(zz * 2 + y, p)
+            pl.when(can_send(up))(lambda: send_z(zz, p, up).start())
+            if to_y:
+                send_y(zz, p).start()
+            if to_x:
+                send_x(zz * 2 + y, p).start()
+
+        remote(d, body)
+
+    def along_y(d, q):
+        def body(sub, zz, up):
+            p = q * SUBS + sub
+            arrived(zz * 2 + 1 - y, p)
+            send_x(zz * 2 + 1 - y, p).start()
+
+        remote(d, body)
+
     load_q.wait()
     load_kv.wait()
-    for q in (role_a, role_b, role_c):
-        pl.when(z < n_z - 1)(lambda q=q: send_z(z, q, True).start())
-        pl.when(z > 0)(lambda q=q: send_z(z, q, False).start())
-        send_y(z, q).start()
-    send_y(z, role_d).start()
+    own_z(role_a, start)
+    own_y(role_a, start)
+    own_z(role_b, start)
     for step in range(1, n_shards):
         send_gain(step).start()
     for s in range(n_shards):
@@ -184,16 +247,18 @@
     load_rows.wait()
     width = own_rows.shape[1]
 
-    def square(i, carry):
+    def square(i):
         rows = pl.ds(pl.multiple_of(i * 32, 32), 32)
         values = own_rows[rows, :].astype(jnp.float32)
         mean = jnp.sum(values * values, axis=1, keepdims=True) / width
         own_inv[rows, :] = jnp.broadcast_to(lax.rsqrt(mean + NORM_EPS), (32, 128))
-        return carry
-
-    lax.fori_loop(0, tokens // 32, square, 0)
+
+    each(tokens // 32, square)
     send_inv.start()
-
+    along_z(1, role_a, True, True)
+
+    for load in load_tables:
+        load.wait()
     n_rows = lengths_ref.shape[0]
     across = lax.broadcasted_iota(jnp.int32, (1, tokens), 1)
     down = lax.broadcasted_iota(jnp.int32, (tokens, 1), 0)
@@ -202,16 +267,16 @@
     start_down = jnp.zeros_like(down)
     target = jnp.zeros_like(across)
     goes_to = jnp.zeros_like(across)
-    start = jnp.int32(0)
+    first = jnp.int32(0)
     for r in range(n_rows):
-        in_across = across >= start
-        in_down = down >= start
+        in_across = across >= first
+        in_down = down >= first
         row_across = jnp.where(in_across, r, row_across)
         row_down = jnp.where(in_down, r, row_down)
-        start_down = jnp.where(in_down, start, start_down)
-        target = jnp.where(in_across, offset_ref[r] + across - start, target)
+        start_down = jnp.where(in_down, first, start_down)
+        target = jnp.where(in_across, offset_ref[r] + across - first, target)
         goes_to = jnp.where(in_across, learner_ref[r], goes_to)
-        start = start + lengths_ref[r]
+        first = first + lengths_ref[r]
     position = (down - start_down).astype(jnp.float32)
     lane = lax.broadcasted_iota(jnp.int32, (1, HD), 1)
     half = HD // 2
@@ -219,6 +284,11 @@
     angle = position * jnp.exp(index * (-2.0 * math.log(ROPE_BASE) / HD))
     cosine[...] = jnp.cos(angle)
     sine[...] = jnp.where(lane < half, -jnp.sin(angle), jnp.sin(angle))
+
+    along_z(1, role_b, True, False)
+    own_y(role_b, start)
+    along_y(1, role_a)
+
     allowed = (row_across == row_down) & (across <= down)
     masked[...] = jnp.where(allowed, 0.0, 1.0)
     if n_dp == 2:
@@ -230,56 +300,35 @@
             slot_iota == jnp.where(goes_to == 1 - dp, target, -1), 1.0, 0.0
         ).astype(jnp.bfloat16)
 
-    def project(slot, first=False):
-        gain = gains[slot][0:1, :]
-        column = pl.multiple_of((slot * 2 + core) * depth, depth)
-        mine = own_rows[:, pl.ds(column, depth)].astype(jnp.float32)
-        normed = (mine * own_inv[:, 0:1] * gain).astype(jnp.bfloat16)
-        result = jnp.dot(normed, weights[slot], preferred_element_type=jnp.float32)
-        total[0] = result if first else total[0] + result
-        theirs = mate_rows[slot].astype(jnp.float32)
-        normed = (theirs * mate_inv[:, 0:1] * gain).astype(jnp.bfloat16)
-        result = jnp.dot(normed, weights[slot], preferred_element_type=jnp.float32)
-        total[1] = result if first else total[1] + result
-
-    def sides(d):
-        return ((z + d < n_z, z + d, False), (z - d >= 0, z - d, True))
-
-    def along_z(d, q, to_y, to_x):
-        for valid, zz, up in sides(d):
-
-            @pl.when(valid)
-            def _(zz=zz, up=up):
-                arrived(zz * 2 + y, q)
-                pl.when(z < n_z - 1 if up else z > 0)(lambda: send_z(zz, q, up).start())
-                if to_y:
-                    send_y(zz, q).start()
-                if to_x:
-                    send_x(zz * 2 + y, q).start()
-
-    def along_y(d, q):
-        for valid, zz, _ in sides(d):
-
-            @pl.when(valid)
-            def _(zz=zz):
-                slot = zz * 2 + 1 - y
-                arrived(slot, q)
-                send_x(slot, q).start()
-
-    def finish(d):
-        for valid, zz, _ in sides(d):
-
-            @pl.when(valid)
-            def _(zz=zz):
-                arrived(zz * 2 + y, role_d)
-                arrived(zz * 2 + 1 - y, role_d)
-                arrived(zz * 2 + 1 - y, role_c)
-
-                def one(i, carry):
-                    project(zz * 2 + i)
-                    return carry
-
-                lax.fori_loop(0, 2, one, 0)
+    block = depth // 2
+
+    def project(slot, h, whose):
+        inner = pl.ds(pl.multiple_of(h * block, block), block)
+        gain = gains[slot, 0:1, inner]
+        if whose == 0:
+            column = pl.multiple_of((slot * 2 + core) * depth + h * block, block)
+            rows, inverse = own_rows[:, pl.ds(column, block)], own_inv[:, 0:1]
+        else:
+            rows, inverse = mate_rows[slot, :, inner], mate_inv[:, 0:1]
+        normed = (rows.astype(jnp.float32) * inverse * gain).astype(jnp.bfloat16)
+        total[whose] += jnp.dot(normed, weights[slot, inner, :], preferred_element_type=jnp.float32)
+
+    def project_both(slot, h):
+        project(slot, h, 1)
+        project(slot, h, 0)
+
+    def project_remote(d, column, h, quarters):
+        def step(up):
+            zz = z + d - 2 * d * up
+
+            @pl.when((zz >= 0) & (zz < n_z))
+            def _():
+                slot = zz * 2 + (y if column == 0 else 1 - y)
+                for q in quarters:
+                    each(SUBS, lambda j: arrived(slot, q * SUBS + j))
+                project_both(slot, h)
+
+        each(2, step)
 
     for step in range(1, n_shards):
         peer = lax.rem(own + step, n_shards)
@@ -291,29 +340,48 @@
             device_id=mate,
             device_id_type=MESH,
         ).wait_recv()
+    along_z(2, role_a, True, True)
+    along_y(1, role_b)
     send_inv.wait_recv()
     for s in range(n_shards):
         send_rows(s).wait_recv()
-
-    along_z(1, role_a, True, True)
-    project(own, first=True)
-    along_z(1, role_b, True, False)
+    total[...] = jnp.zeros_like(total)
+    each(2, lambda h: project_both(own, h))
+    along_z(2, role_b, True, False)
+    own_y(role_c, start)
+    own_z(role_c, start)
+    along_y(2, role_a)
+    for d in range(3, n_z):
+        along_z(d, role_a, True, True)
+        along_y(d - 1, role_b)
+        along_z(d, role_b, True, False)
+        along_y(d, role_a)
+    own_y(role_d, start)
+    project_remote(1, 0, x, ())
     along_z(1, role_c, False, False)
-    for q in range(PIECES):
-        arrived(z * 2 + 1 - y, q)
-    project(z * 2 + 1 - y)
-    for d in range(2, n_z):
-        along_z(d, role_a, True, True)
-        along_y(d - 1, role_a)
-        along_z(d, role_b, True, False)
-        along_y(d - 1, role_b)
+    project_remote(1, 1, x, ())
+    along_y(n_z - 1, role_b)
+    project_remote(2, 0, x, ())
+    along_z(2, role_c, False, False)
+    project_remote(2, 1, x, ())
+    project_remote(1, 1, 1 - x, (role_d, role_c))
+    for d in range(3, n_z):
         along_z(d, role_c, False, False)
-        if d > 2:
-            finish(d - 2)
-    along_y(n_z - 1, role_a)
-    along_y(n_z - 1, role_b)
-    for d in range(max(1, n_z - 2), n_z):
-        finish(d)
+    project_remote(1, 0, 1 - x, (role_d,))
+    project_remote(2, 0, 1 - x, (role_d,))
+    project_remote(2, 1, 1 - x, (role_d, role_c))
+    for d in range(3, n_z):
+        project_remote(d, 0, x, ())
+        project_remote(d, 1, x, ())
+        project_remote(d, 0, 1 - x, (role_d,))
+    for q in (role_a, role_b):
+        each(SUBS, lambda j: arrived(other, q * SUBS + j))
+    project_both(other, x)
+    for d in range(3, n_z):
+        project_remote(d, 1, 1 - x, (role_d, role_c))
+    for q in (role_c, role_d):
+        each(SUBS, lambda j: arrived(other, q * SUBS + j))
+    project(other, 1 - x, 1)
 
     def send_sum(c):
         cols = pl.ds(c * 256, 256)
@@ -330,6 +398,7 @@
     order = [n_sums - 1] + list(range(n_sums - 1))
     for c in order:
         send_sum(c).start()
+    project(other, 1 - x, 0)
 
     def rotated(values):
         return (values * cosine[...] + pltpu.roll(values, half, 1) * sine[...]).astype(jnp.bfloat16)
@@ -375,29 +444,27 @@
             out_ref[:, cols] = mixed
 
     for q in (role_a, role_b, role_c):
-        pl.when(z < n_z - 1)(lambda q=q: send_z(z, q, True).wait_send())
-        pl.when(z > 0)(lambda q=q: send_z(z, q, False).wait_send())
-        send_y(z, q).wait_send()
-    send_y(z, role_d).wait_send()
+        own_z(q, sent)
+    for q in (role_a, role_b, role_c, role_d):
+        own_y(q, sent)
     for step in range(1, n_shards):
         send_gain(step).wait_send()
     for s in range(n_shards):
         send_rows(s).wait_send()
     send_inv.wait_send()
+
+    def relayed(sub, zz, up):
+        a, b, c = (q * SUBS + sub for q in (role_a, role_b, role_c))
+        for p in (a, b, c):
+            pl.when(can_send(up))(lambda p=p: send_z(zz, p, up).wait_send())
+        send_y(zz, a).wait_send()
+        send_y(zz, b).wait_send()
+        send_x(zz * 2 + y, a).wait_send()
+        send_x(zz * 2 + 1 - y, a).wait_send()
+        send_x(zz * 2 + 1 - y, b).wait_send()
+
     for d in range(1, n_z):
-        for valid, zz, up in sides(d):
-
-            @pl.when(valid)
-            def _(zz=zz, up=up):
-                for q in (role_a, role_b, role_c):
-                    pl.when(z < n_z - 1 if up else z > 0)(
-                        lambda q=q: send_z(zz, q, up).wait_send()
-                    )
-                send_y(zz, role_a).wait_send()
-                send_y(zz, role_b).wait_send()
-                send_x(zz * 2 + y, role_a).wait_send()
-                send_x(zz * 2 + 1 - y, role_a).wait_send()
-                send_x(zz * 2 + 1 - y, role_b).wait_send()
+        remote(d, relayed)
 
     for c in order:
         send_sum(c).wait_send()
@@ -418,15 +485,17 @@
     n_shards = 2 * n_z
     bf16, f32 = jnp.bfloat16, jnp.float32
     dma = pltpu.SemaphoreType.DMA
-    smem = pl.BlockSpec(memory_space=pltpu.SMEM)
     vmem = pl.BlockSpec(memory_space=pltpu.VMEM)
     anywhere = pl.BlockSpec(memory_space=pl.ANY)
     return pl.pallas_call(
         functools.partial(kernel, n_dp, n_fsdp),
         out_shape=jax.ShapeDtypeStruct((tokens, q_cols), bf16),
-        in_specs=[smem, smem, smem, anywhere, vmem, anywhere, anywhere],
+        in_specs=[anywhere, anywhere, anywhere, anywhere, vmem, anywhere, anywhere],
         out_specs=vmem,
         scratch_shapes=[
+            pltpu.SMEM(lengths.shape, jnp.int32),
+            pltpu.SMEM(lengths.shape, jnp.int32),
+            pltpu.SMEM(lengths.shape, jnp.int32),
             pltpu.VMEM((n_shards, depth, n_cols), bf16),
             pltpu.VMEM((n_shards, 8, depth), f32),
             pltpu.VMEM((tokens, width), bf16),
@@ -442,11 +511,11 @@
             pltpu.VMEM((tokens, tokens), bf16),
             pltpu.VMEM((QH, tokens, HD), bf16),
             pltpu.VMEM((QH, tokens, HD), bf16),
-            dma((3,)),
-            dma((n_shards, PIECES)),
-            dma((2, n_z, PIECES)),
-            dma((n_z, PIECES)),
-            dma((n_shards, PIECES)),
+            dma((6,)),
+            dma((n_shards, 4 * SUBS)),
+            dma((2, n_z, 4 * SUBS)),
+            dma((n_z, 4 * SUBS)),
+            dma((n_shards, 4 * SUBS)),
             dma((n_shards,)),
             dma((n_shards,)),
             dma((n_shards,)),
@@ -458,9 +527,9 @@
             dma((QH,)),
         ],
         compiler_params=pltpu.CompilerParams(
-            collective_id=0, has_side_effects=True, vmem_limit_bytes=48 * 1024 * 1024
+            collective_id=0, has_side_effects=True, vmem_limit_bytes=60 * 1024 * 1024
         ),
-    )(lengths, learner, slot_offset, hidden, norm_gain.reshape(1, -1), query_weight, keyval_weight)
+    )(lengths, learner, slot_offset, hidden, norm_gain, query_weight, keyval_weight)
 
 
 def route(buffer, tables):

time: 84 us -> 71 us (0.85)
  Pallas kernels: 76.2 us -> 69.1 us
  local copies, waits for them, and re-layouts: 7.53 us -> 1.67 us
    pallas_call x1, Pallas kernels: 76.2 us -> 69.1 us  [fused(): pl.pallas_call(functools.partial(kernel, n_dp, n_fsdp), out_shape=jax.Sha...]
    unnamed x13 -> x1, local copies, waits for them, and re-layouts: 6.85 us -> 1.67 us
where the time goes in v2:
time: 71 us; the launch traced here: 70.8 us
  Pallas kernels  69.1 us (97%)
  local copies, waits for them, and re-layouts  1.67 us (2%)
    pallas_call x1, Pallas kernels, fused(): pl.pallas_call(functools.partial(kernel, n_dp, n_fsdp), out_shape=jax.Sha...  69.1 us
    unnamed x1, local copies, waits for them, and re-layouts  1.67 us

profile of v2, /device:TPU:1, one launch (start us, length us, event | category | flops | bytes accessed | tf_op | source)
XLA Modules:
  0.0 70.8 jit_solution(8362516260608379414)
XLA Ops:
  0.0 69.1 %shard_map.73 = bf16[256,512]{1,0:T(8,128)(2,1)} custom-call(s32[4]{0:T(128)} %lengths_hbm.1, s32[4]{0:T(128)} %learner_hbm.1, s32[4]{0:T(128)} %offset_hbm.1, bf16[256,8192]{1,0:T(8,128)(2,1)} %hidden_ref.1, bf16[512]{0:T(512)(128)(2,1)} %gain_ref.1, bf16[512,512]{1,0:T(8,128)(2,1)} %query_ref.1, bf16[512,256]{1,0:T(8,128)(2,1)} %keyval_ref.1), custom_call_target="tpu_custom_call" | custom-call | tf_op jit(solution)/shard_map/pallas_call | solution.py:490
  69.1 1.7 %copy.9 = bf16[256,512]{1,0:T(8,128)(2,1)} copy(bf16[256,512]{1,0:T(8,128)(2,1)} %shard_map.73) | data formatting | bytes 524288

commit v3 on v2

--- a/solution.py
+++ b/solution.py
@@ -83,6 +83,9 @@
     role_c = 2 - x
     role_d = 3 - 3 * x
 
+    def can_send(up):
+        return (z + 2 * up - 1 >= 0) & (z + 2 * up - 1 < n_z)
+
     load_q = pltpu.make_async_copy(query_ref, weights.at[own, :, pl.ds(0, q_cols)], local_sem.at[0])
     load_kv = pltpu.make_async_copy(
         keyval_ref, weights.at[own, :, pl.ds(q_cols, n_cols - q_cols)], local_sem.at[1]
@@ -103,13 +106,18 @@
     barrier = pltpu.get_barrier_semaphore()
     pl.semaphore_signal(barrier, inc=1, device_id=x_peer, device_id_type=MESH)
     pl.semaphore_signal(barrier, inc=1, device_id=mate, device_id_type=MESH)
-    for step in range(1, n_shards):
-        peer = lax.rem(own + step, n_shards)
-        pl.semaphore_signal(
-            barrier, inc=1, device_id={"fsdp": peer * 2 + core}, device_id_type=MESH
-        )
+    pl.semaphore_signal(barrier, inc=1, device_id=y_peer, device_id_type=MESH)
+    for up in (0, 1):
+
+        @pl.when(can_send(up))
+        def _(up=up):
+            pl.semaphore_signal(
+                barrier, inc=1, device_id={"fsdp": fs + 8 * up - 4}, device_id_type=MESH
+            )
+
     gains[own] = jnp.broadcast_to(gain_ref[...].astype(jnp.float32).reshape(1, depth), (8, depth))
-    pl.semaphore_wait(barrier, n_shards + 1)
+    inner = (z > 0) & (z < n_z - 1)
+    pl.semaphore_wait(barrier, jnp.where(inner, 5, 4))
 
     def piece(slot, p):
         return weights.at[slot, pl.ds(pl.multiple_of(p * part, part), part), :]
@@ -125,9 +133,6 @@
             device_id_type=MESH,
         )
 
-    def can_send(up):
-        return (z + 2 * up - 1 >= 0) & (z + 2 * up - 1 < n_z)
-
     def send_y(zz, p):
         slot = zz * 2 + y
         return pltpu.make_async_remote_copy(
@@ -152,16 +157,32 @@
     def arrived(slot, p):
         send_x(slot, p).wait_recv()
 
-    def send_gain(step):
-        peer = lax.rem(own + step, n_shards)
+    def send_gain(zz, device, sem):
+        slot = zz * 2 + y
         return pltpu.make_async_remote_copy(
-            src_ref=gains.at[own],
-            dst_ref=gains.at[own],
-            send_sem=gain_send.at[step],
-            recv_sem=gain_recv.at[own],
-            device_id={"fsdp": peer * 2 + core},
-            device_id_type=MESH,
-        )
+            src_ref=gains.at[slot],
+            dst_ref=gains.at[slot],
+            send_sem=sem,
+            recv_sem=gain_recv.at[slot],
+            device_id=device,
+            device_id_type=MESH,
+        )
+
+    def gain_z(zz, up):
+        return send_gain(zz, {"fsdp": fs + 8 * up - 4}, gain_send.at[up, zz])
+
+    def gain_y(zz):
+        return send_gain(zz, y_peer, gain_send.at[2, zz])
+
+    def gain_arrived(slot):
+        pltpu.make_async_remote_copy(
+            src_ref=gains.at[slot],
+            dst_ref=gains.at[slot],
+            send_sem=gain_send.at[2, 0],
+            recv_sem=gain_recv.at[slot],
+            device_id=y_peer,
+            device_id_type=MESH,
+        ).wait_recv()
 
     def send_rows(s):
         start = pl.multiple_of((s * 2 + 1 - core) * depth, depth)
@@ -226,6 +247,18 @@
 
         remote(d, body)
 
+    def gain_along_z(d):
+        def step(up):
+            zz = z + d - 2 * d * up
+
+            @pl.when((zz >= 0) & (zz < n_z))
+            def _():
+                gain_arrived(zz * 2 + y)
+                pl.when(can_send(up))(lambda: gain_z(zz, up).start())
+                gain_y(zz).start()
+
+        each(2, step)
+
     def along_y(d, q):
         def body(sub, zz, up):
             p = q * SUBS + sub
@@ -239,10 +272,15 @@
     own_z(role_a, start)
     own_y(role_a, start)
     own_z(role_b, start)
-    for step in range(1, n_shards):
-        send_gain(step).start()
-    for s in range(n_shards):
-        send_rows(s).start()
+    for up in (0, 1):
+        pl.when(can_send(up))(lambda up=up: gain_z(z, up).start())
+    gain_y(z).start()
+
+    def rows_out(i):
+        for k in (2 * i, 2 * i + 1):
+            send_rows(lax.rem(own + k, n_shards)).start()
+
+    rows_out(0)
 
     load_rows.wait()
     width = own_rows.shape[1]
@@ -256,6 +294,8 @@
     each(tokens // 32, square)
     send_inv.start()
     along_z(1, role_a, True, True)
+    gain_along_z(1)
+    rows_out(1)
 
     for load in load_tables:
         load.wait()
@@ -287,7 +327,10 @@
 
     along_z(1, role_b, True, False)
     own_y(role_b, start)
+    rows_out(2)
     along_y(1, role_a)
+    for i in range(3, n_shards // 2):
+        rows_out(i)
 
     allowed = (row_across == row_down) & (across <= down)
     masked[...] = jnp.where(allowed, 0.0, 1.0)
@@ -330,33 +373,27 @@
 
         each(2, step)
 
-    for step in range(1, n_shards):
-        peer = lax.rem(own + step, n_shards)
-        pltpu.make_async_remote_copy(
-            src_ref=gains.at[peer],
-            dst_ref=gains.at[peer],
-            send_sem=gain_send.at[step],
-            recv_sem=gain_recv.at[peer],
-            device_id=mate,
-            device_id_type=MESH,
-        ).wait_recv()
     along_z(2, role_a, True, True)
+    gain_along_z(2)
     along_y(1, role_b)
+    along_z(2, role_b, True, False)
+    own_y(role_c, start)
+    own_z(role_c, start)
     send_inv.wait_recv()
     for s in range(n_shards):
         send_rows(s).wait_recv()
     total[...] = jnp.zeros_like(total)
     each(2, lambda h: project_both(own, h))
-    along_z(2, role_b, True, False)
-    own_y(role_c, start)
-    own_z(role_c, start)
     along_y(2, role_a)
     for d in range(3, n_z):
         along_z(d, role_a, True, True)
+        gain_along_z(d)
         along_y(d - 1, role_b)
         along_z(d, role_b, True, False)
         along_y(d, role_a)
     own_y(role_d, start)
+    for zz in range(n_z):
+        gain_arrived(zz * 2 + 1 - y)
     project_remote(1, 0, x, ())
     along_z(1, role_c, False, False)
     project_remote(1, 1, x, ())
@@ -447,8 +484,10 @@
         own_z(q, sent)
     for q in (role_a, role_b, role_c, role_d):
         own_y(q, sent)
-    for step in range(1, n_shards):
-        send_gain(step).wait_send()
+    for zz in range(n_z):
+        pl.when(can_send(0) & (zz >= z))(lambda zz=zz: gain_z(zz, 0).wait_send())
+        pl.when(can_send(1) & (zz <= z))(lambda zz=zz: gain_z(zz, 1).wait_send())
+        gain_y(zz).wait_send()
     for s in range(n_shards):
         send_rows(s).wait_send()
     send_inv.wait_send()
@@ -486,11 +525,11 @@
     bf16, f32 = jnp.bfloat16, jnp.float32
     dma = pltpu.SemaphoreType.DMA
     vmem = pl.BlockSpec(memory_space=pltpu.VMEM)
-    anywhere = pl.BlockSpec(memory_space=pl.ANY)
+    hbm = pl.BlockSpec(memory_space=pl.ANY)
     return pl.pallas_call(
         functools.partial(kernel, n_dp, n_fsdp),
         out_shape=jax.ShapeDtypeStruct((tokens, q_cols), bf16),
-        in_specs=[anywhere, anywhere, anywhere, anywhere, vmem, anywhere, anywhere],
+        in_specs=[hbm, hbm, hbm, hbm, vmem, hbm, hbm],
         out_specs=vmem,
         scratch_shapes=[
             pltpu.SMEM(lengths.shape, jnp.int32),
@@ -516,7 +555,7 @@
             dma((2, n_z, 4 * SUBS)),
             dma((n_z, 4 * SUBS)),
             dma((n_shards, 4 * SUBS)),
-            dma((n_shards,)),
+            dma((3, n_z)),
             dma((n_shards,)),
             dma((n_shards,)),
             dma((n_shards,)),

time: 71 us -> 71 us (level)
  no operation moved by 1% of the time
where the time goes in v3:
time: 71 us; the launch traced here: 70.8 us
  Pallas kernels  69.1 us (97%)
  local copies, waits for them, and re-layouts  1.67 us (2%)
    pallas_call x1, Pallas kernels, fused(): pl.pallas_call(functools.partial(kernel, n_dp, n_fsdp), out_shape=jax.Sha...  69.1 us
    unnamed x1, local copies, waits for them, and re-layouts  1.67 us

profile of v3, /device:TPU:1, one launch (start us, length us, event | category | flops | bytes accessed | tf_op | source)
XLA Modules:
  0.0 70.8 jit_solution(13415532499066952600)
XLA Ops:
  0.0 69.1 %shard_map.73 = bf16[256,512]{1,0:T(8,128)(2,1)} custom-call(s32[4]{0:T(128)} %lengths_hbm.1, s32[4]{0:T(128)} %learner_hbm.1, s32[4]{0:T(128)} %offset_hbm.1, bf16[256,8192]{1,0:T(8,128)(2,1)} %hidden_ref.1, bf16[512]{0:T(512)(128)(2,1)} %gain_ref.1, bf16[512,512]{1,0:T(8,128)(2,1)} %query_ref.1, bf16[512,256]{1,0:T(8,128)(2,1)} %keyval_ref.1), custom_call_target="tpu_custom_call" | custom-call | tf_op jit(solution)/shard_map/pallas_call | solution.py:529
  69.1 1.7 %copy.9 = bf16[256,512]{1,0:T(8,128)(2,1)} copy(bf16[256,512]{1,0:T(8,128)(2,1)} %shard_map.73) | data formatting | bytes 524288

commit v4 on v3

--- a/solution.py
+++ b/solution.py
@@ -293,8 +293,6 @@
 
     each(tokens // 32, square)
     send_inv.start()
-    along_z(1, role_a, True, True)
-    gain_along_z(1)
     rows_out(1)
 
     for load in load_tables:
@@ -325,10 +323,9 @@
     cosine[...] = jnp.cos(angle)
     sine[...] = jnp.where(lane < half, -jnp.sin(angle), jnp.sin(angle))
 
-    along_z(1, role_b, True, False)
-    own_y(role_b, start)
+    along_z(1, role_a, True, True)
+    gain_along_z(1)
     rows_out(2)
-    along_y(1, role_a)
     for i in range(3, n_shards // 2):
         rows_out(i)
 
@@ -373,47 +370,52 @@
 
         each(2, step)
 
+    along_z(1, role_b, True, False)
+    own_z(role_c, start)
+    own_y(role_b, start)
+    along_y(1, role_a)
     along_z(2, role_a, True, True)
     gain_along_z(2)
     along_y(1, role_b)
-    along_z(2, role_b, True, False)
-    own_y(role_c, start)
-    own_z(role_c, start)
+    total[...] = jnp.zeros_like(total)
     send_inv.wait_recv()
     for s in range(n_shards):
         send_rows(s).wait_recv()
-    total[...] = jnp.zeros_like(total)
-    each(2, lambda h: project_both(own, h))
+    project_both(own, 0)
+    along_z(2, role_b, True, False)
+    own_y(role_c, start)
+    project_both(own, 1)
     along_y(2, role_a)
+    along_z(1, role_c, False, False)
+    project_remote(1, 0, x, ())
     for d in range(3, n_z):
         along_z(d, role_a, True, True)
         gain_along_z(d)
         along_y(d - 1, role_b)
         along_z(d, role_b, True, False)
-        along_y(d, role_a)
+    along_z(2, role_c, False, False)
     own_y(role_d, start)
     for zz in range(n_z):
         gain_arrived(zz * 2 + 1 - y)
-    project_remote(1, 0, x, ())
-    along_z(1, role_c, False, False)
     project_remote(1, 1, x, ())
+    for d in range(3, n_z):
+        along_y(d, role_a)
+    project_remote(2, 0, x, ())
     along_y(n_z - 1, role_b)
-    project_remote(2, 0, x, ())
-    along_z(2, role_c, False, False)
     project_remote(2, 1, x, ())
     project_remote(1, 1, 1 - x, (role_d, role_c))
-    for d in range(3, n_z):
-        along_z(d, role_c, False, False)
     project_remote(1, 0, 1 - x, (role_d,))
-    project_remote(2, 0, 1 - x, (role_d,))
-    project_remote(2, 1, 1 - x, (role_d, role_c))
     for d in range(3, n_z):
         project_remote(d, 0, x, ())
         project_remote(d, 1, x, ())
-        project_remote(d, 0, 1 - x, (role_d,))
+        along_z(d, role_c, False, False)
+    project_remote(2, 0, 1 - x, (role_d,))
+    project_remote(2, 1, 1 - x, (role_d, role_c))
     for q in (role_a, role_b):
         each(SUBS, lambda j: arrived(other, q * SUBS + j))
     project_both(other, x)
+    for d in range(3, n_z):
+        project_remote(d, 0, 1 - x, (role_d,))
     for d in range(3, n_z):
         project_remote(d, 1, 1 - x, (role_d, role_c))
     for q in (role_c, role_d):

time: 71 us -> 67.7 us (0.954)
  Pallas kernels: 69.1 us -> 65.9 us
    pallas_call x1, Pallas kernels: 69.1 us -> 65.9 us  [fused(): pl.pallas_call(functools.partial(kernel, n_dp, n_fsdp), out_shape=jax.Sha...]
where the time goes in v4:
time: 67.7 us; the launch traced here: 67.6 us
  Pallas kernels  65.9 us (97%)
  local copies, waits for them, and re-layouts  1.67 us (2%)
    pallas_call x1, Pallas kernels, fused(): pl.pallas_call(functools.partial(kernel, n_dp, n_fsdp), out_shape=jax.Sha...  65.9 us
    unnamed x1, local copies, waits for them, and re-layouts  1.67 us

profile of v4, /device:TPU:1, one launch (start us, length us, event | category | flops | bytes accessed | tf_op | source)
XLA Modules:
  0.0 67.6 jit_solution(2656654659912152512)
XLA Ops:
  0.0 65.9 %shard_map.73 = bf16[256,512]{1,0:T(8,128)(2,1)} custom-call(s32[4]{0:T(128)} %lengths_hbm.1, s32[4]{0:T(128)} %learner_hbm.1, s32[4]{0:T(128)} %offset_hbm.1, bf16[256,8192]{1,0:T(8,128)(2,1)} %hidden_ref.1, bf16[512]{0:T(512)(128)(2,1)} %gain_ref.1, bf16[512,512]{1,0:T(8,128)(2,1)} %query_ref.1, bf16[512,256]{1,0:T(8,128)(2,1)} %keyval_ref.1), custom_call_target="tpu_custom_call" | custom-call | tf_op jit(solution)/shard_map/pallas_call | solution.py:531
  65.9 1.7 %copy.9 = bf16[256,512]{1,0:T(8,128)(2,1)} copy(bf16[256,512]{1,0:T(8,128)(2,1)} %shard_map.73) | data formatting | bytes 524288

commit v5 on v4

--- a/solution.py
+++ b/solution.py
@@ -37,6 +37,7 @@
     own_inv,
     mate_inv,
     total,
+    sent_sums,
     mate_total,
     cosine,
     sine,
@@ -422,32 +423,34 @@
         each(SUBS, lambda j: arrived(other, q * SUBS + j))
     project(other, 1 - x, 1)
 
-    def send_sum(c):
-        cols = pl.ds(c * 256, 256)
+    groups = ((QH, 2), (0, 1), (1, 1), (2, QH - 2))
+
+    def send_sum(i):
+        first, count = groups[i]
         return pltpu.make_async_remote_copy(
-            src_ref=total.at[1, :, cols],
-            dst_ref=mate_total.at[:, cols],
-            send_sem=sum_send.at[c],
-            recv_sem=sum_recv.at[c],
+            src_ref=sent_sums.at[pl.ds(first, count)],
+            dst_ref=mate_total.at[pl.ds(first, count)],
+            send_sem=sum_send.at[i],
+            recv_sem=sum_recv.at[i],
             device_id=mate,
             device_id_type=MESH,
         )
 
-    n_sums = n_cols // 256
-    order = [n_sums - 1] + list(range(n_sums - 1))
-    for c in order:
-        send_sum(c).start()
+    for i, (first, count) in enumerate(groups):
+        for g in range(first, first + count):
+            sent_sums[g] = total[1, :, g * HD : (g + 1) * HD].astype(jnp.bfloat16)
+        send_sum(i).start()
     project(other, 1 - x, 0)
 
     def rotated(values):
         return (values * cosine[...] + pltpu.roll(values, half, 1) * sine[...]).astype(jnp.bfloat16)
 
-    def summed(col):
-        return total[0, :, col : col + HD] + mate_total[:, col : col + HD]
-
-    send_sum(n_sums - 1).wait_recv()
-    key = rotated(summed(q_cols))
-    value = summed(q_cols + HD).astype(jnp.bfloat16)
+    def summed(g):
+        return total[0, :, g * HD : (g + 1) * HD] + mate_total[g].astype(jnp.float32)
+
+    send_sum(0).wait_recv()
+    key = rotated(summed(QH))
+    value = summed(QH + 1).astype(jnp.bfloat16)
 
     def send_head(h):
         return pltpu.make_async_remote_copy(
@@ -460,9 +463,9 @@
         )
 
     for h in range(QH):
-        if h % 2 == 0:
-            send_sum(h // 2).wait_recv()
-        query = rotated(summed(h * HD))
+        if h < 3:
+            send_sum(h + 1).wait_recv()
+        query = rotated(summed(h))
         scores = lax.dot_general(
             query, key, (((1,), (1,)), ((), ())), preferred_element_type=jnp.float32
         ) * HD ** (-0.5)
@@ -507,8 +510,8 @@
     for d in range(1, n_z):
         remote(d, relayed)
 
-    for c in order:
-        send_sum(c).wait_send()
+    for i in range(len(groups)):
+        send_sum(i).wait_send()
     if n_dp == 2:
         for h in range(QH):
             cols = pl.ds(h * HD, HD)
@@ -544,7 +547,8 @@
             pltpu.VMEM((tokens, 128), f32),
             pltpu.VMEM((tokens, 128), f32),
             pltpu.VMEM((2, tokens, n_cols), f32),
-            pltpu.VMEM((tokens, n_cols), f32),
+            pltpu.VMEM((n_cols // HD, tokens, HD), bf16),
+            pltpu.VMEM((n_cols // HD, tokens, HD), bf16),
             pltpu.VMEM((tokens, HD), f32),
             pltpu.VMEM((tokens, HD), f32),
             pltpu.VMEM((tokens, tokens), f32),
@@ -562,8 +566,8 @@
             dma((n_shards,)),
             dma((n_shards,)),
             dma((2,)),
-            dma((n_cols // 256,)),
-            dma((n_cols // 256,)),
+            dma((4,)),
+            dma((4,)),
             dma((QH,)),
             dma((QH,)),
         ],

time: 67.7 us -> 68.1 us (level)
  no operation moved by 1% of the time
where the time goes in v5:
time: 68.1 us; the launch traced here: 67.6 us
  Pallas kernels  65.9 us (97%)
  local copies, waits for them, and re-layouts  1.67 us (2%)
    pallas_call x1, Pallas kernels, fused(): pl.pallas_call(functools.partial(kernel, n_dp, n_fsdp), out_shape=jax.Sha...  65.9 us
    unnamed x1, local copies, waits for them, and re-layouts  1.67 us

profile of v5, /device:TPU:1, one launch (start us, length us, event | category | flops | bytes accessed | tf_op | source)
XLA Modules:
  0.0 67.6 jit_solution(13242092295116240297)
XLA Ops:
  0.0 65.9 %shard_map.73 = bf16[256,512]{1,0:T(8,128)(2,1)} custom-call(s32[4]{0:T(128)} %lengths_hbm.1, s32[4]{0:T(128)} %learner_hbm.1, s32[4]{0:T(128)} %offset_hbm.1, bf16[256,8192]{1,0:T(8,128)(2,1)} %hidden_ref.1, bf16[512]{0:T(512)(128)(2,1)} %gain_ref.1, bf16[512,512]{1,0:T(8,128)(2,1)} %query_ref.1, bf16[512,256]{1,0:T(8,128)(2,1)} %keyval_ref.1), custom_call_target="tpu_custom_call" | custom-call | tf_op jit(solution)/shard_map/pallas_call | solution.py:534
  65.9 1.7 %copy.9 = bf16[256,512]{1,0:T(8,128)(2,1)} copy(bf16[256,512]{1,0:T(8,128)(2,1)} %shard_map.73) | data formatting | bytes 524288

commit v6 on v4

--- a/solution.py
+++ b/solution.py
@@ -13,7 +13,7 @@
 ROPE_BASE = 500000.0
 NORM_EPS = 1e-05
 MESH = pl.DeviceIdType.MESH
-SUBS = 2
+SUBS = 4
 
 
 def kernel(

time: 67.7 us -> 70.1 us (1.035)
  Pallas kernels: 65.9 us -> 68.2 us
    pallas_call x1, Pallas kernels: 65.9 us -> 68.2 us  [fused(): pl.pallas_call(functools.partial(kernel, n_dp, n_fsdp), out_shape=jax.Sha...]
where the time goes in v6:
time: 70.1 us; the launch traced here: 69.9 us
  Pallas kernels  68.2 us (97%)
  local copies, waits for them, and re-layouts  1.67 us (2%)
    pallas_call x1, Pallas kernels, fused(): pl.pallas_call(functools.partial(kernel, n_dp, n_fsdp), out_shape=jax.Sha...  68.2 us
    unnamed x1, local copies, waits for them, and re-layouts  1.67 us

profile of v6, /device:TPU:1, one launch (start us, length us, event | category | flops | bytes accessed | tf_op | source)
XLA Modules:
  0.0 69.9 jit_solution(18108254144583611466)
XLA Ops:
  0.0 68.2 %shard_map.73 = bf16[256,512]{1,0:T(8,128)(2,1)} custom-call(s32[4]{0:T(128)} %lengths_hbm.1, s32[4]{0:T(128)} %learner_hbm.1, s32[4]{0:T(128)} %offset_hbm.1, bf16[256,8192]{1,0:T(8,128)(2,1)} %hidden_ref.1, bf16[512]{0:T(512)(128)(2,1)} %gain_ref.1, bf16[512,512]{1,0:T(8,128)(2,1)} %query_ref.1, bf16[512,256]{1,0:T(8,128)(2,1)} %keyval_ref.1), custom_call_target="tpu_custom_call" | custom-call | tf_op jit(solution)/shard_map/pallas_call | solution.py:531
  68.2 1.7 %copy.9 = bf16[256,512]{1,0:T(8,128)(2,1)} copy(bf16[256,512]{1,0:T(8,128)(2,1)} %shard_map.73) | data formatting | bytes 524288

commit v7 on v4

--- a/solution.py
+++ b/solution.py
@@ -119,43 +119,43 @@
     inner = (z > 0) & (z < n_z - 1)
     pl.semaphore_wait(barrier, jnp.where(inner, 5, 4))
 
-    def piece(slot, p):
-        return weights.at[slot, pl.ds(pl.multiple_of(p * part, part), part), :]
-
-    def send_z(zz, p, up):
+    def piece(slot, p, n=1):
+        return weights.at[slot, pl.ds(pl.multiple_of(p * part, part), n * part), :]
+
+    def send_z(zz, p, up, n=1):
         slot = zz * 2 + y
         return pltpu.make_async_remote_copy(
-            src_ref=piece(slot, p),
-            dst_ref=piece(slot, p),
+            src_ref=piece(slot, p, n),
+            dst_ref=piece(slot, p, n),
             send_sem=z_send.at[up, zz, p],
             recv_sem=part_recv.at[slot, p],
             device_id={"fsdp": fs + 8 * up - 4},
             device_id_type=MESH,
         )
 
-    def send_y(zz, p):
+    def send_y(zz, p, n=1):
         slot = zz * 2 + y
         return pltpu.make_async_remote_copy(
-            src_ref=piece(slot, p),
-            dst_ref=piece(slot, p),
+            src_ref=piece(slot, p, n),
+            dst_ref=piece(slot, p, n),
             send_sem=y_send.at[zz, p],
             recv_sem=part_recv.at[slot, p],
             device_id=y_peer,
             device_id_type=MESH,
         )
 
-    def send_x(slot, p):
+    def send_x(slot, p, n=1):
         return pltpu.make_async_remote_copy(
-            src_ref=piece(slot, p),
-            dst_ref=piece(slot, p),
+            src_ref=piece(slot, p, n),
+            dst_ref=piece(slot, p, n),
             send_sem=x_send.at[slot, p],
             recv_sem=part_recv.at[slot, p],
             device_id=x_peer,
             device_id_type=MESH,
         )
 
-    def arrived(slot, p):
-        send_x(slot, p).wait_recv()
+    def arrived(slot, p, n=1):
+        send_x(slot, p, n).wait_recv()
 
     def send_gain(zz, device, sem):
         slot = zz * 2 + y
@@ -211,15 +211,15 @@
 
         lax.fori_loop(0, count, step, 0)
 
-    def own_z(q, act):
+    def own_z(q, act, n=1):
         def body(j):
             up = lax.rem(j, 2)
-            pl.when(can_send(up))(lambda: act(send_z(z, q * SUBS + j // 2, up)))
-
-        each(2 * SUBS, body)
-
-    def own_y(q, act):
-        each(SUBS, lambda j: act(send_y(z, q * SUBS + j)))
+            pl.when(can_send(up))(lambda: act(send_z(z, q * SUBS + j // 2, up, n)))
+
+        each(2 * SUBS // n, body)
+
+    def own_y(q, act, n=SUBS):
+        each(SUBS // n, lambda j: act(send_y(z, q * SUBS + j, n)))
 
     def start(copy):
         copy.start()
@@ -227,25 +227,25 @@
     def sent(copy):
         copy.wait_send()
 
-    def remote(d, body):
+    def remote(d, body, subs=SUBS):
         def step(j):
             up = lax.rem(j, 2)
             zz = z + d - 2 * d * up
             pl.when((zz >= 0) & (zz < n_z))(lambda: body(j // 2, zz, up))
 
-        each(2 * SUBS, step)
-
-    def along_z(d, q, to_y, to_x):
+        each(2 * subs, step)
+
+    def along_z(d, q, to_y, to_x, n=1):
         def body(sub, zz, up):
             p = q * SUBS + sub
-            arrived(zz * 2 + y, p)
-            pl.when(can_send(up))(lambda: send_z(zz, p, up).start())
+            arrived(zz * 2 + y, p, n)
+            pl.when(can_send(up))(lambda: send_z(zz, p, up, n).start())
             if to_y:
                 send_y(zz, p).start()
             if to_x:
                 send_x(zz * 2 + y, p).start()
 
-        remote(d, body)
+        remote(d, body, SUBS // n)
 
     def gain_along_z(d):
         def step(up):
@@ -270,7 +270,7 @@
     load_q.wait()
     load_kv.wait()
     own_z(role_a, start)
-    own_y(role_a, start)
+    own_y(role_a, start, 1)
     own_z(role_b, start)
     for up in (0, 1):
         pl.when(can_send(up))(lambda up=up: gain_z(z, up).start())
@@ -371,7 +371,7 @@
         each(2, step)
 
     along_z(1, role_b, True, False)
-    own_z(role_c, start)
+    own_z(role_c, start, SUBS)
     own_y(role_b, start)
     along_y(1, role_a)
     along_z(2, role_a, True, True)
@@ -386,14 +386,14 @@
     own_y(role_c, start)
     project_both(own, 1)
     along_y(2, role_a)
-    along_z(1, role_c, False, False)
+    along_z(1, role_c, False, False, SUBS)
     project_remote(1, 0, x, ())
     for d in range(3, n_z):
         along_z(d, role_a, True, True)
         gain_along_z(d)
         along_y(d - 1, role_b)
         along_z(d, role_b, True, False)
-    along_z(2, role_c, False, False)
+    along_z(2, role_c, False, False, SUBS)
     own_y(role_d, start)
     for zz in range(n_z):
         gain_arrived(zz * 2 + 1 - y)
@@ -408,18 +408,18 @@
     for d in range(3, n_z):
         project_remote(d, 0, x, ())
         project_remote(d, 1, x, ())
-        along_z(d, role_c, False, False)
+        along_z(d, role_c, False, False, SUBS)
     project_remote(2, 0, 1 - x, (role_d,))
     project_remote(2, 1, 1 - x, (role_d, role_c))
-    for q in (role_a, role_b):
-        each(SUBS, lambda j: arrived(other, q * SUBS + j))
+    each(SUBS, lambda j: arrived(other, role_a * SUBS + j))
+    arrived(other, role_b * SUBS, SUBS)
     project_both(other, x)
     for d in range(3, n_z):
         project_remote(d, 0, 1 - x, (role_d,))
     for d in range(3, n_z):
         project_remote(d, 1, 1 - x, (role_d, role_c))
     for q in (role_c, role_d):
-        each(SUBS, lambda j: arrived(other, q * SUBS + j))
+        arrived(other, q * SUBS, SUBS)
     project(other, 1 - x, 1)
 
     def send_sum(c):
@@ -482,9 +482,11 @@
         else:
             out_ref[:, cols] = mixed
 
-    for q in (role_a, role_b, role_c):
+    for q in (role_a, role_b):
         own_z(q, sent)
-    for q in (role_a, role_b, role_c, role_d):
+    own_z(role_c, sent, SUBS)
+    own_y(role_a, sent, 1)
+    for q in (role_b, role_c, role_d):
         own_y(q, sent)
     for zz in range(n_z):
         pl.when(can_send(0) & (zz >= z))(lambda zz=zz: gain_z(zz, 0).wait_send())
@@ -495,8 +497,8 @@
     send_inv.wait_send()
 
     def relayed(sub, zz, up):
-        a, b, c = (q * SUBS + sub for q in (role_a, role_b, role_c))
-        for p in (a, b, c):
+        a, b = role_a * SUBS + sub, role_b * SUBS + sub
+        for p in (a, b):
             pl.when(can_send(up))(lambda p=p: send_z(zz, p, up).wait_send())
         send_y(zz, a).wait_send()
         send_y(zz, b).wait_send()
@@ -504,8 +506,12 @@
         send_x(zz * 2 + 1 - y, a).wait_send()
         send_x(zz * 2 + 1 - y, b).wait_send()
 
+    def relayed_whole(sub, zz, up):
+        pl.when(can_send(up))(lambda: send_z(zz, role_c * SUBS, up, SUBS).wait_send())
+
     for d in range(1, n_z):
         remote(d, relayed)
+        remote(d, relayed_whole, 1)
 
     for c in order:
         send_sum(c).wait_send()

time: 67.7 us -> 67.6 us (level)
  no operation moved by 1% of the time
where the time goes in v7:
time: 67.6 us; the launch traced here: 67.5 us
  Pallas kernels  65.8 us (97%)
  local copies, waits for them, and re-layouts  1.67 us (2%)
    pallas_call x1, Pallas kernels, fused(): pl.pallas_call(functools.partial(kernel, n_dp, n_fsdp), out_shape=jax.Sha...  65.8 us
    unnamed x1, local copies, waits for them, and re-layouts  1.67 us

profile of v7, /device:TPU:1, one launch (start us, length us, event | category | flops | bytes accessed | tf_op | source)
XLA Modules:
  0.0 67.5 jit_solution(9004608427917286626)
XLA Ops:
  0.0 65.8 %shard_map.73 = bf16[256,512]{1,0:T(8,128)(2,1)} custom-call(s32[4]{0:T(128)} %lengths_hbm.1, s32[4]{0:T(128)} %learner_hbm.1, s32[4]{0:T(128)} %offset_hbm.1, bf16[256,8192]{1,0:T(8,128)(2,1)} %hidden_ref.1, bf16[512]{0:T(512)(128)(2,1)} %gain_ref.1, bf16[512,512]{1,0:T(8,128)(2,1)} %query_ref.1, bf16[512,256]{1,0:T(8,128)(2,1)} %keyval_ref.1), custom_call_target="tpu_custom_call" | custom-call | tf_op jit(solution)/shard_map/pallas_call | solution.py:537
  65.8 1.7 %copy.9 = bf16[256,512]{1,0:T(8,128)(2,1)} copy(bf16[256,512]{1,0:T(8,128)(2,1)} %shard_map.73) | data formatting | bytes 524288

commit v8 on v7

--- a/solution.py
+++ b/solution.py
@@ -342,7 +342,7 @@
 
     block = depth // 2
 
-    def project(slot, h, whose):
+    def normed(slot, h, whose):
         inner = pl.ds(pl.multiple_of(h * block, block), block)
         gain = gains[slot, 0:1, inner]
         if whose == 0:
@@ -350,12 +350,18 @@
             rows, inverse = own_rows[:, pl.ds(column, block)], own_inv[:, 0:1]
         else:
             rows, inverse = mate_rows[slot, :, inner], mate_inv[:, 0:1]
-        normed = (rows.astype(jnp.float32) * inverse * gain).astype(jnp.bfloat16)
-        total[whose] += jnp.dot(normed, weights[slot, inner, :], preferred_element_type=jnp.float32)
+        return (rows.astype(jnp.float32) * inverse * gain).astype(jnp.bfloat16)
+
+    def product(rows, slot, h):
+        inner = pl.ds(pl.multiple_of(h * block, block), block)
+        return jnp.dot(rows, weights[slot, inner, :], preferred_element_type=jnp.float32)
+
+    def project(slot, h, whose):
+        total[whose] += product(normed(slot, h, whose), slot, h)
 
     def project_both(slot, h):
-        project(slot, h, 1)
-        project(slot, h, 0)
+        rows = jnp.concatenate([normed(slot, h, 0), normed(slot, h, 1)], axis=0)
+        total[...] += product(rows, slot, h).reshape(total.shape)
 
     def project_remote(d, column, h, quarters):
         def step(up):

time: 67.6 us -> 67.7 us (level)
  no operation moved by 1% of the time
where the time goes in v8:
time: 67.7 us; the launch traced here: 67.5 us
  Pallas kernels  65.9 us (97%)
  local copies, waits for them, and re-layouts  1.67 us (2%)
    pallas_call x1, Pallas kernels, fused(): pl.pallas_call(functools.partial(kernel, n_dp, n_fsdp), out_shape=jax.Sha...  65.9 us
    unnamed x1, local copies, waits for them, and re-layouts  1.67 us

profile of v8, /device:TPU:1, one launch (start us, length us, event | category | flops | bytes accessed | tf_op | source)
XLA Modules:
  0.0 67.5 jit_solution(9204750109375470241)
XLA Ops:
  0.0 65.9 %shard_map.73 = bf16[256,512]{1,0:T(8,128)(2,1)} custom-call(s32[4]{0:T(128)} %lengths_hbm.1, s32[4]{0:T(128)} %learner_hbm.1, s32[4]{0:T(128)} %offset_hbm.1, bf16[256,8192]{1,0:T(8,128)(2,1)} %hidden_ref.1, bf16[512]{0:T(512)(128)(2,1)} %gain_ref.1, bf16[512,512]{1,0:T(8,128)(2,1)} %query_ref.1, bf16[512,256]{1,0:T(8,128)(2,1)} %keyval_ref.1), custom_call_target="tpu_custom_call" | custom-call | tf_op jit(solution)/shard_map/pallas_call | solution.py:543
  65.9 1.7 %copy.9 = bf16[256,512]{1,0:T(8,128)(2,1)} copy(bf16[256,512]{1,0:T(8,128)(2,1)} %shard_map.73) | data formatting | bytes 524288

commit v9 on v7

--- a/solution.py
+++ b/solution.py
@@ -13,7 +13,7 @@
 ROPE_BASE = 500000.0
 NORM_EPS = 1e-05
 MESH = pl.DeviceIdType.MESH
-SUBS = 2
+SUBS = 1
 
 
 def kernel(

time: 67.6 us -> 67.2 us (level)
  no operation moved by 1% of the time
where the time goes in v9:
time: 67.2 us; the launch traced here: 67 us
  Pallas kernels  65.3 us (97%)
  local copies, waits for them, and re-layouts  1.67 us (2%)
    pallas_call x1, Pallas kernels, fused(): pl.pallas_call(functools.partial(kernel, n_dp, n_fsdp), out_shape=jax.Sha...  65.3 us
    unnamed x1, local copies, waits for them, and re-layouts  1.67 us

profile of v9, /device:TPU:1, one launch (start us, length us, event | category | flops | bytes accessed | tf_op | source)
XLA Modules:
  0.0 67.0 jit_solution(18311283456243883188)
XLA Ops:
  0.0 65.3 %shard_map.73 = bf16[256,512]{1,0:T(8,128)(2,1)} custom-call(s32[4]{0:T(128)} %lengths_hbm.1, s32[4]{0:T(128)} %learner_hbm.1, s32[4]{0:T(128)} %offset_hbm.1, bf16[256,8192]{1,0:T(8,128)(2,1)} %hidden_ref.1, bf16[512]{0:T(512)(128)(2,1)} %gain_ref.1, bf16[512,512]{1,0:T(8,128)(2,1)} %query_ref.1, bf16[512,256]{1,0:T(8,128)(2,1)} %keyval_ref.1), custom_call_target="tpu_custom_call" | custom-call | tf_op jit(solution)/shard_map/pallas_call | solution.py:537
  65.4 1.7 %copy.9 = bf16[256,512]{1,0:T(8,128)(2,1)} copy(bf16[256,512]{1,0:T(8,128)(2,1)} %shard_map.73) | data formatting | bytes 524288
